TPU v7x, 128 devices: a whole 4x4x4 slice. The times are simulated.
128 devices in a mesh: tm: 16 (over x, z), rows: 8 (over y, core).
Axes of the slice: x: 4, y: 4, z: 4, core: 2. Of those that a mesh axis runs over, the one named last changes fastest.
Arguments:
- video: bfloat16 [256, 32, 32, 512], P('tm', 'rows'), may hold values from -6 to 6
- video_ids: int32 [256], replicated, may hold values from 0 to 15, never falling along the last dimension, each value on 1 to 32 neighbouring positions
- w_space: bfloat16 [9, 512, 512], replicated, may hold values from -0.09375 to 0.09375
- w_time: bfloat16 [3, 512, 512], replicated, may hold values from -0.15625 to 0.15625
- spatial_attn: bfloat16 [4, 512, 512], replicated, may hold values from -2 to 2, as said below
- time_attn: bfloat16 [4, 512, 512], replicated, may hold values from -2 to 2, as said below
Outputs:
- mixed: bfloat16 [256, 32, 32, 512], P(None, 'rows', 'tm')
Inputs may be any that keep to these rules, and one draw needn't show every extreme that they name: `spatial_attn`: Query, key, value and output projections stacked in this order. `time_attn`: Query, key, value and output projections stacked in this order.
All inputs are finite; a program needn't handle non-finite values.
Results may differ from a plain program's by a relative error of at most 0.024.
The roundings to bfloat16 on the way count: a program that leaves them out, or rounds other values in their place, can miss the bound.
Values may be sent and summed in bfloat16 or wider, within the bound.
No kernel may reach another device: no remote copies, remote signals or barrier semaphores. Data moves between devices by JAX's collectives and lax.ppermute only.
A program may use at most 128 MiB of HBM per device.

v0:
```python
import jax
import jax.numpy as jnp
from jax import lax
from jax.sharding import PartitionSpec as P

GROUPS = 32


epsilon = 1e-06
masked_score = -1e30


def with_halo(shard, sides, width):
    for axis, dim in sides:
        size, length = (lax.axis_size(axis), shard.shape[dim])
        up = [(i, (i + 1) % size) for i in range(size - 1)]
        down = [(j, i) for i, j in up]
        last = lax.slice_in_dim(shard, length - width, length, axis=dim)
        leading = lax.slice_in_dim(shard, 0, width, axis=dim)
        before = lax.ppermute(last, axis, up)
        after = lax.ppermute(leading, axis, down)
        shard = jnp.concatenate([before, shard, after], axis=dim)
    return shard


def from_behind(block, axis, distance):
    devices = range(lax.axis_size(axis))
    route = [(i - distance, i) for i in devices if i - distance in devices]
    return lax.ppermute(block, axis, route)


def space_conv(padded, weights):
    frame_count, height_ext, col_count, channel_width = padded.shape
    row_count = height_ext - 2
    widened = jnp.pad(padded, ((0, 0), (0, 0), (1, 1), (0, 0)))
    summed = jnp.zeros((frame_count * row_count * col_count, channel_width), jnp.float32)
    for row_shift in range(3):
        for col_shift in range(3):
            window = widened[
                :, row_shift : row_shift + row_count, col_shift : col_shift + col_count, :
            ]
            summed = summed + jnp.dot(
                window.reshape(-1, channel_width),
                weights[row_shift * 3 + col_shift],
                preferred_element_type=jnp.float32,
            )
    return summed.reshape(frame_count, row_count, col_count, channel_width)


def group_totals(values, groups):
    batch_size, length, channel_width = values.shape
    group_sums = jnp.sum(values, axis=1).reshape(batch_size, groups, -1).sum(axis=2)
    squares = jnp.sum(values * values, axis=1).reshape(batch_size, groups, -1).sum(axis=2)
    return (group_sums, squares)


def normalize(values, group_sums, squares, entries, groups):
    channel_width = values.shape[-1]
    per_group = channel_width // groups
    average = group_sums / entries
    spread = squares / entries - average * average
    inverse = lax.rsqrt(spread + epsilon)
    average_full = jnp.repeat(average, per_group, axis=1)[:, None, :]
    inverse_full = jnp.repeat(inverse, per_group, axis=1)[:, None, :]
    return ((values - average_full) * inverse_full).astype(jnp.bfloat16)


def project(normed, weights):
    shape_in = normed.shape
    channel_width = shape_in[-1]
    flattened = normed.reshape(-1, channel_width)
    outputs = [
        jnp.dot(flattened, weights[index], preferred_element_type=jnp.float32)
        .astype(jnp.bfloat16)
        .reshape(shape_in)
        for index in range(3)
    ]
    return (outputs[0], outputs[1], outputs[2])


def finish(tokens, query_rows, gathered_keys, gathered_values, weights):
    channel_width = tokens.shape[-1]
    attention_logits = jnp.einsum(
        "edm,efm->edf", query_rows, gathered_keys, preferred_element_type=jnp.float32
    ) * channel_width ** (-0.5)
    top = jnp.max(attention_logits, axis=-1, keepdims=True)
    raised = jnp.exp(attention_logits - top)
    attention_probs = (raised / jnp.sum(raised, axis=-1, keepdims=True)).astype(jnp.bfloat16)
    mixed_output = jnp.einsum(
        "lup,lpe->lue", attention_probs, gathered_values, preferred_element_type=jnp.float32
    ).astype(jnp.bfloat16)
    output = tokens.astype(jnp.float32) + jnp.dot(
        mixed_output.reshape(-1, channel_width), weights[3], preferred_element_type=jnp.float32
    ).reshape(tokens.shape)
    return output.astype(jnp.bfloat16)


def time_attention(column_block, video_ids, weights):
    frame_total, positions, channel_width = column_block.shape
    values = column_block.astype(jnp.float32)
    average = jnp.mean(values, axis=-1, keepdims=True)
    centered = values - average
    spread = jnp.mean(centered * centered, axis=-1, keepdims=True)
    normed = (centered * lax.rsqrt(spread + epsilon)).astype(jnp.bfloat16)
    query_rows, resident_keys, resident_values = project(normed, weights)
    attention_logits = jnp.einsum(
        "fpc,gpc->pfg", query_rows, resident_keys, preferred_element_type=jnp.float32
    ) * channel_width ** (-0.5)
    frame_index = jnp.arange(frame_total, dtype=jnp.int32)
    allowed = (frame_index[None, :] <= frame_index[:, None]) & (
        video_ids[None, :] == video_ids[:, None]
    )
    attention_logits = jnp.where(allowed[None], attention_logits, masked_score)
    top = jnp.max(attention_logits, axis=-1, keepdims=True)
    raised = jnp.exp(attention_logits - top)
    attention_probs = (raised / jnp.sum(raised, axis=-1, keepdims=True)).astype(jnp.bfloat16)
    mixed_output = jnp.einsum(
        "pfg,gpc->fpc", attention_probs, resident_values, preferred_element_type=jnp.float32
    ).astype(jnp.bfloat16)
    output = values + jnp.dot(
        mixed_output.reshape(-1, channel_width), weights[3], preferred_element_type=jnp.float32
    ).reshape(column_block.shape)
    return output.astype(jnp.bfloat16)


def shards(video, video_ids, w_space, w_time, spatial_attn, time_attn):
    frame_count, row_count, col_count, channel_width = video.shape
    tm_count = lax.axis_size("tm")
    rows_count = lax.axis_size("rows")
    padded = with_halo(video, (("rows", 1),), 1)
    hidden = jax.nn.silu(space_conv(padded, w_space)).astype(jnp.bfloat16)
    earlier = from_behind(hidden[frame_count - 2 :], "tm", 1)
    extended = jnp.concatenate([earlier, hidden], axis=0)
    span_index = lax.axis_index("tm")
    ids_padded = jnp.concatenate([jnp.full((2,), -1, jnp.int32), video_ids])
    local_ids = lax.dynamic_slice_in_dim(ids_padded, span_index * frame_count, frame_count + 2)
    same_one = (local_ids[1 : frame_count + 1] == local_ids[2:])[:, None, None, None]
    same_two = (local_ids[:frame_count] == local_ids[2:])[:, None, None, None]
    prev_one = jnp.where(same_one, extended[1 : frame_count + 1], hidden)
    prev_two = jnp.where(same_two, extended[:frame_count], prev_one)
    temporal = jnp.dot(
        hidden.reshape(-1, channel_width), w_time[0], preferred_element_type=jnp.float32
    )
    temporal = temporal + jnp.dot(
        prev_one.reshape(-1, channel_width), w_time[1], preferred_element_type=jnp.float32
    )
    temporal = temporal + jnp.dot(
        prev_two.reshape(-1, channel_width), w_time[2], preferred_element_type=jnp.float32
    )
    conv_out = (video.astype(jnp.float32) + temporal.reshape(video.shape)).astype(jnp.bfloat16)
    per_group = channel_width // GROUPS
    frames = lax.all_to_all(conv_out, "rows", split_axis=0, concat_axis=1, tiled=True)
    whole_count, height, col_total, channels_in = frames.shape
    tokens = frames.reshape(whole_count, height * col_total, channel_width)
    values = tokens.astype(jnp.float32)
    group_sums, squares = group_totals(values, GROUPS)
    normed = normalize(values, group_sums, squares, tokens.shape[1] * per_group, GROUPS)
    query_rows, resident_keys, resident_values = project(normed, spatial_attn)
    frame_out = finish(tokens, query_rows, resident_keys, resident_values, spatial_attn).reshape(
        frames.shape
    )
    row_slab = height // rows_count
    col_slab = col_total // tm_count
    arrived = lax.all_to_all(
        lax.all_to_all(frame_out, "tm", split_axis=2, concat_axis=0, tiled=True),
        "rows",
        split_axis=1,
        concat_axis=0,
        tiled=True,
    )
    arrived = arrived.reshape(rows_count, tm_count, whole_count, row_slab, col_slab, channel_width)
    by_time = jnp.swapaxes(arrived, 0, 1).reshape(
        rows_count * tm_count * whole_count, row_slab, col_slab, channel_width
    )
    frame_total = by_time.shape[0]
    flattened = by_time.reshape(frame_total, -1, channel_width)
    return time_attention(flattened, video_ids, time_attn).reshape(by_time.shape)


def solution(mesh):
    in_specs = (P("tm", "rows", None, None), P(), P(), P(), P(), P())
    out_specs = P(None, "rows", "tm", None)
    return jax.shard_map(shards, mesh=mesh, in_specs=in_specs, out_specs=out_specs, check_vma=False)
```

profile of v0, /device:TPU:1, one launch (start us, length us, event | category | flops | bytes accessed | tf_op | source)
XLA Modules:
  0.0 265.5 jit_solution(2899877513540470104)
XLA Ops:
  0.0 2.4 fusion.111
  2.4 4.6 %collective-permute-start = (bf16[16,1,32,512]{3,2,1,0:T(8,128)(2,1)}, bf16[16,1,32,512]{3,2,1,0:T(8,128)(2,1)S(1)}, u32[]{:S(2)}, u32[]{:S(2)}) collective-permute-start(bf16[16,1,32,512]{3,2,1,0:T(8,128)(2,1)} %get-tuple-element.17), channel_id=1, source_target_pairs={{0,1},{1,2},{2,3},{3,4},{4,5},{5,6},{6,7},{8,9},{9,10},{10,11},{11... | collective-permute-start | bytes 1572872 | tf_op jit(solution)/shard_map/ppermute | solution.py:20
  7.0 1.9 collective-permute-start.1
  9.1 2.3 fusion.64
  11.4 2.0 collective-permute-done
  13.4 4.3 %collective-permute-done.1 = bf16[16,1,32,512]{3,2,1,0:T(8,128)(2,1)S(1)} collective-permute-done((bf16[16,1,32,512]{3,2,1,0:T(8,128)(2,1)}, bf16[16,1,32,512]{3,2,1,0:T(8,128)(2,1)S(1)}, u32[]{:S(2)}, u32[]{:S(2)}) %collective-permute-start.1) | collective-permute-done | bytes 524320 | tf_op jit(solution)/shard_map/ppermute | solution.py:21
  17.7 2.0 fusion.16
  19.7 5.5 %fusion.110 = (bf16[16,4,32,512]{3,2,1,0:T(8,128)(2,1)}, bf16[16,4,32,512]{3,2,1,0:T(8,128)(2,1)S(1)}, bf16[16,4,32,512]{3,2,1,0:T(8,128)(2,1)S(1)}, bf16[16,4,3...) fusion(bf16[16,6,34,512]{3,2,1,0:T(8,128)(2,1)S(1)} %fusion.16), kind=kLoop, calls=%fused_computation.134 | loop fusion | bytes 25165824 | tf_op jit(solution)/shard_map/slice | solution.py:39
  25.2 2.4 fusion.60
  27.7 4.3 %fusion.62 = f32[2048,512]{1,0:T(8,128)} fusion(bf16[2048,512]{1,0:T(8,128)(2,1)S(1)} %bitcast.156, bf16[9,512,512]{2,1,0:T(8,128)(2,1)} %param.8), kind=kOutput, calls=%fused_computation.85 | convolution fusion | flops 1073741824 | bytes 6815744 | tf_op jit(solution)/shard_map/dot_general | solution.py:42
  32.0 3.2 %fusion.66 = f32[2048,512]{1,0:T(8,128)} fusion(bf16[2048,512]{1,0:T(8,128)(2,1)S(1)} %bitcast.155, bf16[9,512,512]{2,1,0:T(8,128)(2,1)S(1)} %bitcast.167), kind=kOutput, calls=%fused_computation.89 | convolution fusion | flops 1073741824 | bytes 6815744 | tf_op jit(solution)/shard_map/dot_general | solution.py:42
  35.2 3.2 %fusion.68 = f32[2048,512]{1,0:T(8,128)} fusion(bf16[2048,512]{1,0:T(8,128)(2,1)S(1)} %bitcast.154, bf16[9,512,512]{2,1,0:T(8,128)(2,1)S(1)} %bitcast.167), kind=kOutput, calls=%fused_computation.91 | convolution fusion | flops 1073741824 | bytes 6815744 | tf_op jit(solution)/shard_map/dot_general | solution.py:42
  38.4 3.2 %fusion.72 = f32[2048,512]{1,0:T(8,128)} fusion(bf16[2048,512]{1,0:T(8,128)(2,1)S(1)} %bitcast.153, bf16[9,512,512]{2,1,0:T(8,128)(2,1)S(1)} %bitcast.167), kind=kOutput, calls=%fused_computation.95 | convolution fusion | flops 1073741824 | bytes 6815744 | tf_op jit(solution)/shard_map/dot_general | solution.py:42
  41.6 0.3 pad_maximum_fusion.2
  41.9 3.2 %fusion.58 = f32[2048,512]{1,0:T(8,128)} fusion(bf16[2048,512]{1,0:T(8,128)(2,1)S(1)} %bitcast.159, bf16[9,512,512]{2,1,0:T(8,128)(2,1)S(1)} %bitcast.167), kind=kOutput, calls=%fused_computation.81 | convolution fusion | flops 1073741824 | bytes 6815744 | tf_op jit(solution)/shard_map/dot_general | solution.py:42
  45.2 3.2 %fusion.70 = f32[2048,512]{1,0:T(8,128)} fusion(bf16[2048,512]{1,0:T(8,128)(2,1)S(1)} %bitcast.158, bf16[9,512,512]{2,1,0:T(8,128)(2,1)S(1)} %bitcast.167), kind=kOutput, calls=%fused_computation.93 | convolution fusion | flops 1073741824 | bytes 6815744 | tf_op jit(solution)/shard_map/dot_general | solution.py:42
  48.4 13.2 %add_add_fusion.1 = f32[2048,512]{1,0:T(8,128)} fusion(f32[2048,512]{1,0:T(8,128)} %fusion.58, f32[2048,512]{1,0:T(8,128)S(1)} %fusion.60, f32[2048,512]{1,0:T(8,128)} %fusion.62, f32[2048,512]{1,0:T(8,128)S(1)} %fusion.64, f32[2048,512]{1,0:T(8,128)} %fusion.66, f32[2048,512]{1,0:T(8,128)} %fusion.68, f32[2048,512]{1,0:T(8,128)} %fusion.72, ...), kind=kOutput, calls=%fused_computation.29 | convolution fusion | flops 1082130432 | bytes 40370176 | tf_op jit(solution)/shard_map/dot_general | solution.py:42
  61.6 3.4 %multiply_convert_fusion.1 = bf16[16,4,32,512]{3,2,1,0:T(8,128)(2,1)S(1)} fusion(f32[16,4,32,512]{3,2,1,0:T(8,128)} %bitcast.151), kind=kLoop, calls=%fused_computation.27 | loop fusion | flops 5242880 | bytes 6291456 | tf_op jit(solution)/shard_map/convert_element_type | solution.py:131
  65.1 3.6 %collective-permute-start.2 = (bf16[2,4,32,512]{3,2,1,0:T(8,128)(2,1)S(1)}, bf16[2,4,32,512]{3,2,1,0:T(8,128)(2,1)S(1)}, u32[]{:S(2)}, u32[]{:S(2)}) collective-permute-start(bf16[2,4,32,512]{3,2,1,0:T(8,128)(2,1)S(1)} %slice.157), channel_id=1, source_target_pairs={{0,8},{8,16},{16,24},{24,32},{32,40},{40,48},{48,56},{56,64},{64,7... | collective-permute-start | bytes 786440 | tf_op jit(solution)/shard_map/ppermute | solution.py:29
  68.7 1.3 fusion.28
  70.0 1.9 collective-permute-done.2
  71.9 1.3 fusion.19
  73.3 1.3 fusion.51
  74.6 1.5 add_add_fusion
  76.1 0.9 add_convert_fusion.1
  77.0 32.9 %all_to_all.39 = bf16[16,4,32,512]{3,2,1,0:T(8,128)(2,1)S(1)} all-to-all(bf16[16,4,32,512]{3,2,1,0:T(8,128)(2,1)S(1)} %add_convert_fusion.1), channel_id=1, replica_groups=mesh['tm'=16,'rows'=8] {'rows'}, dimensions={0} | all-to-all | bytes 4194304 | tf_op jit(solution)/shard_map/all_to_all | solution.py:152
  109.9 0.6 bitcast_convert_fusion
  110.5 0.6 bitcast_reduce_fusion
  111.5 0.1 mul.76
  111.8 0.6 copy.45
  112.4 0.6 fusion.10
  113.0 1.5 copy-done.5
  114.5 1.0 copy-done.9
  115.5 1.3 convolution_convert_fusion.5
  116.8 2.6 convolution_convert_fusion.4
  119.4 2.6 convolution_convert_fusion.3
  121.9 8.5 %fusion.112 = (f32[2,1024]{1,0:T(2,128)S(1)}, f32[2,1024,1024]{1,2,0:T(8,128)}) fusion(bf16[2,1024,512]{2,1,0:T(8,128)(2,1)S(1)} %bitcast.174, bf16[2,1024,512]{2,1,0:T(8,128)(2,1)} %bitcast.175), kind=kOutput, calls=%fused_computation.136 | convolution fusion | flops 2153776128 | bytes 12591104 | tf_op jit(solution)/shard_map/sub | solution.py:87
  130.5 8.8 %fusion.11 = bf16[2,1024,512]{2,1,0:T(8,128)(2,1)S(1)} fusion(f32[8,2,4,32,512]{4,3,2,0,1:T(8,128)} %copy-done.5, bf16[2,1024,512]{2,1,0:T(8,128)(2,1)} %bitcast.173, f32[2,1024,1024]{1,2,0:T(8,128)} %get-tuple-element.24, f32[2,1024]{1,0:T(2,128)S(1)} %get-tuple-element.23, bf16[4,512,512]{2,1,0:T(8,128)(2,1)} %param.10), kind=kOutput, calls=%fused_computation.17 | convolution fusion | flops 3228565504 | bytes 17309696 | tf_op jit(solution)/shard_map/dot_general | solution.py:92
  139.3 1.3 copy.47
  140.6 33.7 %all_to_all.40 = bf16[2,32,32,512]{3,1,0,2:T(8,128)(2,1)S(1)} all-to-all(bf16[2,32,32,512]{3,1,0,2:T(8,128)(2,1)S(1)} %copy.47), channel_id=1, replica_groups=mesh['tm'=16,'rows'=8] {'tm'}, dimensions={2} | all-to-all | bytes 4194304 | tf_op jit(solution)/shard_map/all_to_all | solution.py:165
  174.3 0.1 copy.49
  174.5 3.5 %copy.50 = bf16[32,32,2,512]{3,2,0,1:T(2,128)(2,1)} copy(bf16[32,32,2,512]{3,1,2,0:T(8,128)(2,1)S(1)} %bitcast.164) | data formatting | bytes 4194304 | tf_op jit(solution)/shard_map/all_to_all | solution.py:165
  178.0 6.9 %all-to-all-start.2 = ((bf16[32,32,2,512]{3,2,0,1:T(2,128)(2,1)}), bf16[32,32,2,512]{3,2,0,1:T(2,128)(2,1)S(1)}, u32[]{:S(2)}, u32[]{:S(2)}) async-start(bf16[32,32,2,512]{3,2,0,1:T(2,128)(2,1)} %copy.50), calls=%async_computation.2 | async-start | bytes 4194304 | tf_op jit(solution)/shard_map/all_to_all | solution.py:164
  184.9 0.1 fusion.94
  185.0 26.2 %all-to-all-done.2 = bf16[32,32,2,512]{3,2,0,1:T(2,128)(2,1)S(1)} async-done(((bf16[32,32,2,512]{3,2,0,1:T(2,128)(2,1)}), bf16[32,32,2,512]{3,2,0,1:T(2,128)(2,1)S(1)}, u32[]{:S(2)}, u32[]{:S(2)}) %all-to-all-start.2) | async-done | bytes 2097184 | tf_op jit(solution)/shard_map/all_to_all | solution.py:164
  211.3 0.5 copy.51
  211.8 0.6 convert_bitcast_fusion
  212.3 4.4 %copy.52 = f32[8,32,4,2,512]{4,0,3,2,1:T(8,128)} copy(f32[8,32,4,2,512]{4,1,3,2,0:T(8,128)S(1)} %convert_bitcast_fusion) | data formatting | bytes 8388608 | tf_op jit(solution)/shard_map/convert_element_type | solution.py:100
  216.7 2.6 reduce_sum.77
  219.4 3.1 %multiply_reduce_fusion.1 = f32[16,8,2,4,2]{1,4,3,2,0:T(2,128)S(1)} fusion(f32[16,8,2,4,2,512]{5,1,4,3,2,0:T(8,128)} %bitcast.147, f32[16,8,2,4,2]{1,4,3,2,0:T(2,128)S(1)} %broadcast_multiply_fusion), kind=kLoop, calls=%fused_computation.23 | loop fusion | flops 3143680 | bytes 4210688 | tf_op jit(solution)/shard_map/reduce_sum | solution.py:103
  222.6 0.2 copy-done.3
  222.8 2.4 multiply_convert_fusion
  225.3 2.2 copy.54
  227.5 2.4 convert_element_type.168
  230.0 3.1 %fusion.35 = bf16[256,8,512]{2,1,0:T(8,128)(2,1)S(1)} fusion(bf16[2048,512]{1,0:T(8,128)(2,1)} %convert_element_type.168, bf16[4,512,512]{2,1,0:T(8,128)(2,1)} %param.11), kind=kOutput, calls=%fused_computation.61 | convolution fusion | flops 1074790400 | bytes 4718592 | tf_op jit(solution)/shard_map/dot_general | solution.py:73
  233.1 2.6 fusion.36
  235.7 2.6 fusion.34
  238.3 6.0 %copy.53 = f32[16,8,2,4,2,512]{5,2,1,0,4,3:T(2,128)} copy(f32[16,8,2,4,2,512]{5,1,4,3,2,0:T(8,128)S(1)} %bitcast.148) | data formatting | bytes 8388608 | tf_op jit(solution)/shard_map/convert_element_type | solution.py:100
  244.3 6.3 %reshape.262 = f32[256,8,512]{2,0,1:T(8,128)} reshape(f32[16,8,2,4,2,512]{5,2,1,0,4,3:T(2,128)} %copy.53) | data formatting | bytes 8388608 | tf_op jit(solution)/shard_map/convert_element_type | solution.py:100
  250.6 2.9 %fusion.23 = f32[8,256,256]{1,2,0:T(8,128)S(1)} fusion(bf16[256,8,512]{2,1,0:T(8,128)(2,1)} %fusion.36, bf16[256,8,512]{2,1,0:T(8,128)(2,1)S(1)} %fusion.35), kind=kOutput, calls=%fused_computation.50 | convolution fusion | flops 536870912 | bytes 6291456 | tf_op jit(solution)/shard_map/fpc,gpc->pfg/dot_general | solution.py:106
  253.5 1.3 copy-done.11
  254.8 0.6 fusion.113
  255.4 6.4 %add_convert_fusion = bf16[256,8,512]{2,0,1:T(8,128)(2,1)S(1)} fusion(f32[256,8,512]{2,0,1:T(8,128)} %reshape.262, bf16[256,8,512]{2,1,0:T(8,128)(2,1)} %fusion.34, f32[8,256]{1,0:T(8,128)S(1)} %fusion.113, bf16[4,512,512]{2,1,0:T(8,128)(2,1)} %param.11, f32[8,256,256]{1,2,0:T(8,128)} %copy-done.11, pred[256,256]{0,1:T(8,128)(4,1)S(1)} %fusion.94), kind=kOutput, calls=%fused_computation.21 | convolution fusion | flops 1616382208 | bytes 11083776 | tf_op jit(solution)/shard_map/dot_general | solution.py:120
  261.8 3.5 %copy.60 = bf16[256,4,2,512]{3,2,1,0:T(2,128)(2,1)} copy(bf16[256,4,2,512]{3,0,2,1:T(8,128)(2,1)S(1)} %bitcast.168) | data formatting | bytes 4194304 | tf_op jit(solution)/shard_map/reshape | solution.py:177
  (38 shorter events, 1.0 us)
Async XLA Ops:
  0.0 9.1 %copy-start.1 = (bf16[16,4,32,512]{3,2,1,0:T(8,128)(2,1)S(1)}, bf16[16,4,32,512]{3,2,1,0:T(8,128)(2,1)}, u32[]{:S(2)}) copy-start(bf16[16,4,32,512]{3,2,1,0:T(8,128)(2,1)} %param.6) | copy-start | bytes 6291460
  0.0 9.0 %copy-start.8 = (s32[256]{0:T(256)S(1)}, s32[256]{0:T(256)}, u32[]{:S(2)}) copy-start(s32[256]{0:T(256)} %param.7) | copy-start | bytes 3076
  2.4 11.0 %collective-permute-start = (bf16[16,1,32,512]{3,2,1,0:T(8,128)(2,1)}, bf16[16,1,32,512]{3,2,1,0:T(8,128)(2,1)S(1)}, u32[]{:S(2)}, u32[]{:S(2)}) collective-permute-start(bf16[16,1,32,512]{3,2,1,0:T(8,128)(2,1)} %get-tuple-element.17), channel_id=1, source_target_pairs={{0,1},{1,2},{2,3},{3,4},{4,5},{5,6},{6,7},{8,9},{9,10},{10,11},{11... | collective-permute-start | bytes 1572872 | tf_op jit(solution)/shard_map/ppermute | solution.py:20
  7.0 10.7 %collective-permute-start.1 = (bf16[16,1,32,512]{3,2,1,0:T(8,128)(2,1)}, bf16[16,1,32,512]{3,2,1,0:T(8,128)(2,1)S(1)}, u32[]{:S(2)}, u32[]{:S(2)}) collective-permute-start(bf16[16,1,32,512]{3,2,1,0:T(8,128)(2,1)} %get-tuple-element.18), channel_id=1, source_target_pairs={{1,0},{2,1},{3,2},{4,3},{5,4},{6,5},{7,6},{9,8},{10,9},{11,10},{12... | collective-permute-start | bytes 1572872 | tf_op jit(solution)/shard_map/ppermute | solution.py:21
  25.2 6.7 %slice-start = ((s8[4718592]{0:T(1024)(128)(4,1)}), s8[4194304]{0:T(1024)(128)(4,1)S(1)}, s32[]{:S(2)}) async-start(s8[4718592]{0:T(1024)(128)(4,1)} %bitcast.166), calls=%async_computation.3 | async-start | bytes 8388608
  27.7 4.3 %slice-start.1 = ((s8[4718592]{0:T(1024)(128)(4,1)}), s8[524288]{0:T(1024)(128)(4,1)S(1)}, s32[]{:S(2)}) async-start(s8[4718592]{0:T(1024)(128)(4,1)} %bitcast.166), calls=%async_computation.4 | async-start | bytes 1048576
  61.6 7.0 %copy-start.4 = (f32[2048,512]{1,0:T(8,128)S(1)}, f32[2048,512]{1,0:T(8,128)}, u32[]{:S(2)}) copy-start(f32[2048,512]{1,0:T(8,128)} %add_add_fusion.1) | copy-start | bytes 12582916
  61.6 7.1 %copy-start.7 = (bf16[3,512,512]{2,1,0:T(8,128)(2,1)S(1)}, bf16[3,512,512]{2,1,0:T(8,128)(2,1)}, u32[]{:S(2)}) copy-start(bf16[3,512,512]{2,1,0:T(8,128)(2,1)} %param.9) | copy-start | bytes 4718596
  65.1 6.8 %collective-permute-start.2 = (bf16[2,4,32,512]{3,2,1,0:T(8,128)(2,1)S(1)}, bf16[2,4,32,512]{3,2,1,0:T(8,128)(2,1)S(1)}, u32[]{:S(2)}, u32[]{:S(2)}) collective-permute-start(bf16[2,4,32,512]{3,2,1,0:T(8,128)(2,1)S(1)} %slice.157), channel_id=1, source_target_pairs={{0,8},{8,16},{16,24},{24,32},{32,40},{40,48},{48,56},{56,64},{64,7... | collective-permute-start | bytes 786440 | tf_op jit(solution)/shard_map/ppermute | solution.py:29
  112.4 2.1 copy-start.5
  112.4 3.1 %copy-start.9 = (bf16[4,512,512]{2,1,0:T(8,128)(2,1)S(1)}, bf16[4,512,512]{2,1,0:T(8,128)(2,1)}, u32[]{:S(2)}) copy-start(bf16[4,512,512]{2,1,0:T(8,128)(2,1)} %param.10) | copy-start | bytes 6291460
  178.0 33.3 %all-to-all-start.2 = ((bf16[32,32,2,512]{3,2,0,1:T(2,128)(2,1)}), bf16[32,32,2,512]{3,2,0,1:T(2,128)(2,1)S(1)}, u32[]{:S(2)}, u32[]{:S(2)}) async-start(bf16[32,32,2,512]{3,2,0,1:T(2,128)(2,1)} %copy.50), calls=%async_computation.2 | async-start | bytes 4194304 | tf_op jit(solution)/shard_map/all_to_all | solution.py:164
  212.3 4.4 %copy-start.2 = (f32[8,32,4,2,512]{4,1,3,2,0:T(8,128)}, f32[8,32,4,2,512]{4,1,3,2,0:T(8,128)S(1)}, u32[]{:S(2)}) copy-start(f32[8,32,4,2,512]{4,1,3,2,0:T(8,128)S(1)} %convert_bitcast_fusion) | copy-start | bytes 12582916
  219.4 3.5 %copy-start.3 = (f32[8,32,4,2,512]{4,1,3,2,0:T(8,128)S(1)}, f32[8,32,4,2,512]{4,1,3,2,0:T(8,128)}, u32[]{:S(2)}) copy-start(f32[8,32,4,2,512]{4,1,3,2,0:T(8,128)} %copy-done.2) | copy-start | bytes 12582916
  229.9 3.1 %copy-start.6 = (bf16[2048,512]{1,0:T(8,128)(2,1)S(1)}, bf16[2048,512]{1,0:T(8,128)(2,1)}, u32[]{:S(2)}) copy-start(bf16[2048,512]{1,0:T(8,128)(2,1)} %convert_element_type.168) | copy-start | bytes 6291460
  229.9 3.1 %copy-start.10 = (bf16[4,512,512]{2,1,0:T(8,128)(2,1)S(1)}, bf16[4,512,512]{2,1,0:T(8,128)(2,1)}, u32[]{:S(2)}) copy-start(bf16[4,512,512]{2,1,0:T(8,128)(2,1)} %param.11) | copy-start | bytes 6291460
  235.7 2.6 copy-start
  253.5 1.3 copy-start.11
where the time goes:
time: 270 us; the launch traced here: 266 us
  matrix products  83.8 us (31%)
  blocking collectives  66.6 us (25%)
  local copies, waits for them, and re-layouts  43.4 us (16%)
  waiting for transfers between devices  34.5 us (13%)
  other arithmetic  19.6 us (7%)
  starting transfers between devices  17 us (6%)
    dot_general x9, matrix products, space_conv(): jnp.dot(window.reshape(-1, channel_width), weights[row_shift * 3 + col_sh...  38.3 us
    all_to_all x1, blocking collectives, shards(): lax.all_to_all(frame_out, 'tm', split_axis=2, concat_axis=0, tiled=True)  33.7 us
    all_to_all x1, blocking collectives, shards(): lax.all_to_all(conv_out, 'rows', split_axis=0, concat_axis=1, tiled=True)  32.9 us
    all_to_all x1, waiting for transfers between devices, shards(): lax.all_to_all(lax.all_to_all(frame_out, 'tm', split_axis=2, concat_axis=...  26.2 us
    convert_element_type x3, local copies, waits for them, and re-layouts, time_attention(): values = column_block.astype(jnp.float32)  16.7 us
    dot_general x6, matrix products, project(): jnp.dot(flattened, weights[index], preferred_element_type=jnp.float32)  14.7 us
    dot_general x1, matrix products, finish(): jnp.dot(mixed_output.reshape(-1, channel_width), weights[3], preferred_el...  8.83 us
    sub x1, matrix products, finish(): raised = jnp.exp(attention_logits - top)  8.53 us
  transfers between devices with their start and end apart: 4, of which 4 were waited for; matrix products, arithmetic and copies ran while one was open for 1% of the time, Pallas kernels for 0%

commit v1 on v0

v1 whole, which is shorter than its diff:
```python
import functools

import jax
import jax.numpy as jnp
import numpy as np
from jax import lax
from jax.experimental import pallas as pl
from jax.experimental.pallas import tpu as pltpu
from jax.sharding import PartitionSpec as P

GROUPS = 32
EPS = 1e-06
MASKED = -1e30
LOG2E = 1.4426950408889634
BF = jnp.bfloat16
F32 = jnp.float32
VMEM_LIMIT = 56 * 1024 * 1024


def mm(a, b):
    return jnp.dot(a, b, preferred_element_type=F32)


def mm_nt(a, b):
    return lax.dot_general(a, b, (((1,), (1,)), ((), ())), preferred_element_type=F32)


def one_hot_rows(n, source_of):
    out_row = lax.broadcasted_iota(jnp.int32, (n, n), 0)
    in_row = lax.broadcasted_iota(jnp.int32, (n, n), 1)
    return jnp.where(in_row == source_of(out_row), 1.0, 0.0).astype(BF)


def conv_kernel(first, frames, idx_ref, *refs):
    if first:
        (x_ref, up_ref, dn_ref, xp_ref, upp_ref, dnp_ref, w_ref, wt_ref,
         out_ref, tail_ref, ext, acc, hs) = refs
        lead = 2
    else:
        (x_ref, up_ref, dn_ref, hp_ref, w_ref, wt_ref, out_ref, ext, acc, hs) = refs
        lead = 0
    total = frames + lead
    per = 5 if total % 5 == 0 else 4
    rows = per * 128
    step = pl.program_id(0)
    c = x_ref.shape[-1]

    @pl.when(step == 0)
    def _():
        if first:
            ext[0:2, 0:32, :] = upp_ref[...]
            ext[0:2, 32:160, :] = xp_ref[...]
            ext[0:2, 160:192, :] = dnp_ref[...]
        else:
            hs[0:2] = hp_ref[...]
        ext[lead:total, 0:32, :] = up_ref[...]
        ext[lead:total, 32:160, :] = x_ref[...]
        ext[lead:total, 160:192, :] = dn_ref[...]

    def tap(block):
        f0 = block * per
        lhs = jnp.concatenate(
            [ext[f0 : f0 + per, 32 * a : 32 * a + 128, :].reshape(rows, c) for a in range(3)], axis=1
        )
        return mm(lhs, w_ref[:, 0].reshape(3 * c, c))

    def col_is(value):
        row = lax.broadcasted_iota(jnp.int32, (rows, c), 0)
        return (row & 31) == value

    @pl.when(step == 0)
    def _():
        for block in range(total // per):
            y = tap(block)
            acc[block * rows : (block + 1) * rows] = jnp.where(col_is(0), 0.0, pltpu.roll(y, 1, 0))

    @pl.when(step == 1)
    def _():
        for block in range(total // per):
            acc[block * rows : (block + 1) * rows] += tap(block)

    @pl.when(step == 2)
    def _():
        for block in range(total // per):
            y = tap(block)
            y = jnp.where(col_is(31), 0.0, pltpu.roll(y, rows - 1, 0))
            v = acc[block * rows : (block + 1) * rows] + y
            half = 0.5 * v
            hidden = (half + half * jnp.tanh(half)).astype(BF)
            f0 = block * per + 2 - lead
            hs[f0 : f0 + per] = hidden.reshape(per, 128, c)

    @pl.when(step == 3)
    def _():
        order = one_hot_rows(128, lambda o: ((o >> 1) & 3) * 32 + (o >> 3) * 2 + (o & 1))
        weights = wt_ref[...].reshape(3 * c, c)
        per_t = 4
        for f0 in range(0, frames, per_t):
            now = hs[f0 + 2 : f0 + 2 + per_t].reshape(per_t * 128, c)
            one = jnp.concatenate([hs[idx_ref[0, f0 + k]] for k in range(per_t)], axis=0)
            two = jnp.concatenate([hs[idx_ref[1, f0 + k]] for k in range(per_t)], axis=0)
            y = mm(jnp.concatenate([now, one, two], axis=1), weights)
            y = y + x_ref[f0 : f0 + per_t].reshape(per_t * 128, c).astype(F32)
            y = y.astype(BF)
            for k in range(per_t):
                out_ref[f0 + k] = mm(order, y[k * 128 : (k + 1) * 128]).astype(BF)
        if first:
            tail_ref[...] = hs[frames : frames + 2]


def conv_chunk(first, idx, x, halos, w_space, w_time):
    frames, tokens, c = x.shape
    total = frames + (2 if first else 0)
    whole = lambda a: pl.BlockSpec(a.shape, lambda s, i, n=a.ndim: (0,) * n)
    ins = [x, *halos]
    in_specs = [whole(a) for a in ins]
    in_specs.append(pl.BlockSpec((3, 1, c, c), lambda s, i: (0, jnp.minimum(s, 2), 0, 0)))
    in_specs.append(whole(w_time))
    out_shape = [jax.ShapeDtypeStruct((frames, tokens, c), BF)]
    if first:
        out_shape.append(jax.ShapeDtypeStruct((2, tokens, c), BF))
    flops = 2 * total * tokens * 9 * c * c + 2 * frames * tokens * 3 * c * c
    return pl.pallas_call(
        functools.partial(conv_kernel, first, frames),
        out_shape=out_shape,
        grid_spec=pltpu.PrefetchScalarGridSpec(
            num_scalar_prefetch=1,
            grid=(4,),
            in_specs=in_specs,
            out_specs=[whole(o) for o in out_shape],
            scratch_shapes=[
                pltpu.VMEM((total, 192, c), BF),
                pltpu.VMEM((total * tokens, c), F32),
                pltpu.VMEM((frames + 2, tokens, c), BF),
            ],
        ),
        compiler_params=pltpu.CompilerParams(
            dimension_semantics=("arbitrary",), vmem_limit_bytes=VMEM_LIMIT
        ),
        cost_estimate=pl.CostEstimate(flops=flops, bytes_accessed=9 * 2**20, transcendentals=0),
        name="conv_chunk",
    )(idx, *ins, w_space.reshape(3, 3, c, c), w_time)


def softmax_rows(scores, scale):
    top = jnp.max(scores, axis=-1, keepdims=True)
    raised = jnp.exp2((scores - top) * scale)
    return (raised * (1.0 / jnp.sum(raised, axis=-1, keepdims=True))).astype(BF)


def group_sum(v, per_group):
    lane = lax.broadcasted_iota(jnp.int32, v.shape, 1)
    n = v.shape[1]
    d = 1
    while d < per_group:
        v = v + jnp.where((lane & d) == 0, pltpu.roll(v, n - d, 1), pltpu.roll(v, d, 1))
        d *= 2
    return v


def frame_kernel(x_ref, xq_ref, w_ref, out_ref, q_s, k_s, v_s):
    step = pl.program_id(0)
    tokens, c = x_ref.shape
    tile = out_ref.shape[0]

    @pl.when(step == 0)
    def _():
        values = x_ref[...].astype(F32)
        sums = jnp.sum(values, axis=0, keepdims=True)
        squares = jnp.sum(values * values, axis=0, keepdims=True)
        per_group = c // GROUPS
        entries = tokens * per_group
        both = group_sum(jnp.concatenate([sums, squares] * 4, axis=0), per_group) / entries
        average, square = both[0:1], both[1:2]
        inverse = lax.rsqrt(square - average * average + EPS)
        normed = ((values - average) * inverse).astype(BF)
        q_s[...] = mm(normed, w_ref[0]).astype(BF)
        k_s[...] = mm(normed, w_ref[1]).astype(BF)
        v_s[...] = mm(normed, w_ref[2]).astype(BF)

    q = q_s[pl.ds(step * tile, tile), :]
    probs = softmax_rows(mm_nt(q, k_s[...]), c ** (-0.5) * LOG2E)
    mix = mm(probs, v_s[...]).astype(BF)
    out_ref[...] = (xq_ref[...].astype(F32) + mm(mix, w_ref[3])).astype(BF)


def frame_attention(x, weights):
    tokens, c = x.shape
    tile = 256
    return pl.pallas_call(
        frame_kernel,
        out_shape=jax.ShapeDtypeStruct((tokens, c), BF),
        grid=(tokens // tile,),
        in_specs=[
            pl.BlockSpec((tokens, c), lambda s: (0, 0)),
            pl.BlockSpec((tile, c), lambda s: (s, 0)),
            pl.BlockSpec(weights.shape, lambda s: (0, 0, 0)),
        ],
        out_specs=pl.BlockSpec((tile, c), lambda s: (s, 0)),
        scratch_shapes=[pltpu.VMEM((tokens, c), BF)] * 3,
        compiler_params=pltpu.CompilerParams(
            dimension_semantics=("arbitrary",), vmem_limit_bytes=VMEM_LIMIT
        ),
        cost_estimate=pl.CostEstimate(
            flops=8 * tokens * c * c + 4 * tokens * tokens * c,
            bytes_accessed=5 * 2**20,
            transcendentals=tokens * tokens,
        ),
        name="frame_attention",
    )(x, x, weights)


def by_cell(o):
    return (o & 7) * 32 + ((o >> 3) & 3) * 8 + (o >> 5)


def by_frame(o):
    return (o & 7) * 32 + (o >> 3)


def cell_rows(block, order):
    return mm(order, block).astype(BF)


def project_time(x, w_ref):
    values = x.astype(F32)
    average = jnp.mean(values, axis=-1, keepdims=True)
    centered = values - average
    spread = jnp.mean(centered * centered, axis=-1, keepdims=True)
    normed = (centered * lax.rsqrt(spread + EPS)).astype(BF)
    return [mm(normed, w_ref[i]).astype(BF) for i in range(3)]


def qkv_kernel(x_ref, w_ref, xo_ref, q_ref, k_ref, v_ref):
    c = x_ref.shape[-1]
    order = one_hot_rows(256, by_cell)
    x = cell_rows(x_ref[...].reshape(256, c), order)
    q, k, v = project_time(x, w_ref)
    for ref, value in ((xo_ref, x), (q_ref, q), (k_ref, k), (v_ref, v)):
        ref[...] = value.reshape(8, 32, c)


def time_qkv(x, weights):
    r, tc, c = x.shape
    out = jax.ShapeDtypeStruct((8, r * tc // 8, c), BF)
    block = pl.BlockSpec((8, 32, c), lambda s: (0, s, 0))
    return pl.pallas_call(
        qkv_kernel,
        out_shape=[out] * 4,
        grid=(tc // 32,),
        in_specs=[block, pl.BlockSpec(weights.shape, lambda s: (0, 0, 0))],
        out_specs=[block] * 4,
        compiler_params=pltpu.CompilerParams(
            dimension_semantics=("arbitrary",), vmem_limit_bytes=VMEM_LIMIT
        ),
        cost_estimate=pl.CostEstimate(
            flops=6 * r * tc * c * c, bytes_accessed=7 * 2**20, transcendentals=0
        ),
        name="time_qkv",
    )(x, weights)


def time_kernel(x1_ref, bias_ref, w_ref, x0_hbm, q0_hbm, k0_hbm, v0_hbm, out_ref, x_s, q_s, k_s, v_s, m_s, sems):
    c = x1_ref.shape[-1]
    scratch = (x_s, q_s, k_s, v_s)
    copies = [
        pltpu.make_async_copy(src, dst.at[:, 0:128], sems.at[i])
        for i, (src, dst) in enumerate(zip((x0_hbm, q0_hbm, k0_hbm, v0_hbm), scratch))
    ]
    for copy in copies:
        copy.start()
    order = one_hot_rows(256, by_cell)
    for u in range(4):
        x = cell_rows(x1_ref[:, 32 * u : 32 * u + 32, :].reshape(256, c), order)
        for ref, value in zip(scratch, [x, *project_time(x, w_ref)]):
            ref[:, 128 + 32 * u : 160 + 32 * u, :] = value.reshape(8, 32, c)
    for copy in copies:
        copy.wait()
    for cell in range(8):
        scores = mm_nt(q_s[cell], k_s[cell]) * (c ** (-0.5) * LOG2E) + bias_ref[...]
        m_s[cell] = mm(softmax_rows(scores, 1.0), v_s[cell]).astype(BF)
    back = one_hot_rows(256, by_frame)
    for chunk in range(2):
        for u in range(4):
            f0 = chunk * 128 + 32 * u
            y = mm(m_s[:, f0 : f0 + 32, :].reshape(256, c), w_ref[3])
            y = (y + x_s[:, f0 : f0 + 32, :].reshape(256, c).astype(F32)).astype(BF)
            y = mm(back, y).astype(BF)
            out_ref[4 * u : 4 * u + 4, chunk * 64 : chunk * 64 + 64, :] = y.reshape(4, 64, c)


def time_finish(x1, bias, weights, parts):
    r, tc, c = x1.shape
    vmem = pl.BlockSpec(memory_space=pltpu.VMEM)
    hbm = pl.BlockSpec(memory_space=pl.ANY)
    return pl.pallas_call(
        time_kernel,
        out_shape=jax.ShapeDtypeStruct((16, 128, c), BF),
        in_specs=[vmem] * 3 + [hbm] * 4,
        out_specs=vmem,
        scratch_shapes=[pltpu.VMEM((8, 256, c), BF)] * 5 + [pltpu.SemaphoreType.DMA((4,))],
        compiler_params=pltpu.CompilerParams(vmem_limit_bytes=VMEM_LIMIT),
        cost_estimate=pl.CostEstimate(
            flops=6 * r * tc * c * c + 4 * r * tc * c * c + 8 * 4 * 256 * 256 * c,
            bytes_accessed=10 * 2**20,
            transcendentals=8 * 256 * 256,
        ),
        name="time_finish",
    )(x1, bias, weights, *parts)


def shards(video, video_ids, w_space, w_time, spatial_attn, time_attn):
    frames, rows, cols, c = video.shape
    tm_count, rows_count = lax.axis_size("tm"), lax.axis_size("rows")
    half = frames // 2
    up = [(i, i + 1) for i in range(rows_count - 1)]
    down = [(i + 1, i) for i in range(rows_count - 1)]
    span = [(t, t + 1) for t in range(tm_count - 1)]
    both = ("tm", "rows")
    tokens = rows * cols
    flat = lambda a: a.reshape(a.shape[0], -1, c)

    top, bottom = video[:, 0], video[:, rows - 1]
    late = frames - 2
    halos = [
        (lax.ppermute(bottom[k : k + half], "rows", up), lax.ppermute(top[k : k + half], "rows", down))
        for k in (0, half)
    ]
    prev = lax.ppermute(video[late:], "tm", span)
    diag = lambda moves: [(a * rows_count + i, b * rows_count + j) for a, b in span for i, j in moves]
    prev_up = lax.ppermute(bottom[late:], both, diag(up))
    prev_dn = lax.ppermute(top[late:], both, diag(down))

    ids = jnp.concatenate([jnp.full((2,), -1, jnp.int32), video_ids])
    ids = lax.dynamic_slice_in_dim(ids, lax.axis_index("tm") * frames, frames + 2)
    place = jnp.arange(frames, dtype=jnp.int32) % half
    one = jnp.where(ids[1:-1] == ids[2:], place + 1, place + 2)
    two = jnp.where(ids[:-2] == ids[2:], place, one)
    idx = jnp.stack([one, two])

    x = flat(video)
    conv0, tail = conv_chunk(
        True, idx[:, :half], x[:half], [*halos[0], flat(prev), prev_up, prev_dn], w_space, w_time
    )
    (conv1,) = conv_chunk(False, idx[:, half:], x[half:], [*halos[1], tail], w_space, w_time)

    arrived = []
    for conv in (conv0, conv1):
        frame = lax.all_to_all(conv, "rows", 0, 0, tiled=True).reshape(rows_count * tokens, c)
        out = frame_attention(frame, spatial_attn)
        arrived.append(
            lax.all_to_all(out, ("rows", "tm"), 0, 0, tiled=True).reshape(rows_count, -1, c)
        )

    order = np.arange(frames * tm_count).reshape(tm_count, 2, half).transpose(1, 0, 2).reshape(-1)
    ids_here = video_ids.reshape(tm_count, 2, half).transpose(1, 0, 2).reshape(-1)
    number = jnp.asarray(order, jnp.int32)
    allowed = (number[None, :] <= number[:, None]) & (ids_here[None, :] == ids_here[:, None])
    bias = jnp.where(allowed, 0.0, MASKED).astype(F32)

    parts = time_qkv(arrived[0], time_attn)
    out = time_finish(arrived[1], bias, time_attn, parts)
    return out.reshape(frames * tm_count, rows, cols // tm_count, c)


def solution(mesh):
    in_specs = (P("tm", "rows", None, None), P(), P(), P(), P(), P())
    out_specs = P(None, "rows", "tm", None)
    return jax.shard_map(shards, mesh=mesh, in_specs=in_specs, out_specs=out_specs, check_vma=False)
```

time: 270 us -> 160 us (0.59); the launches traced: 266 us -> 159 us
  matrix products: 83.8 us -> 0 us
  blocking collectives: 66.6 us -> 0 us
  Pallas kernels: 0 us -> 64.5 us
  local copies, waits for them, and re-layouts: 43.4 us -> 12.4 us
  starting transfers between devices: 17 us -> 45.4 us
  other arithmetic: 19.6 us -> 0.94 us
    dot_general x21 -> x0, matrix products: 75.2 us -> none  [the longest x9 38.3 us: space_conv(): jnp.dot(window.reshape(-1, channel_width), weights[row_shift * 3 + col_sh...]
    all_to_all x2 -> x0, blocking collectives: 66.6 us -> none  [the longest x1 33.7 us: shards(): lax.all_to_all(frame_out, 'tm', split_axis=2, concat_axis=0, tiled=True)]
    pallas_call x0 -> x6, Pallas kernels: none -> 64.5 us  [the longest x2 25.7 us: conv_chunk(): pl.pallas_call(functools.partial(conv_kernel, first, frames), out_shape=o...]
    convert_element_type x6 -> x0, local copies, waits for them, and re-layouts: 21.9 us -> none  [the longest x3 16.7 us: time_attention(): values = column_block.astype(jnp.float32)]
    all_to_all x1 -> x4, starting transfers between devices: 6.94 us -> 22 us  [the longest x2 11.9 us: shards(): lax.all_to_all(out, ('rows', 'tm'), 0, 0, tiled=True)]
    ppermute x3 -> x7, starting transfers between devices: 10.1 us -> 23.5 us  [the longest x2 7.24 us: shards(): lax.ppermute(bottom[k:k + half], 'rows', up)]
    convert_element_type x6 -> x0, other arithmetic: 8.57 us -> none  [the longest x1 3.44 us: shards(): hidden = jax.nn.silu(space_conv(padded, w_space)).astype(jnp.bfloat16)]
    sub x1 -> x0, matrix products: 8.53 us -> none  [finish(): raised = jnp.exp(attention_logits - top)]
  transfers between devices with their start and end apart: 4 -> 11, of which waited for: 4 -> 5; matrix products, arithmetic and copies ran while one was open for 1% -> 4% of each run, Pallas kernels for 0% -> 25%
where the time goes in v1:
time: 160 us; the launch traced here: 159 us
  Pallas kernels  64.5 us (40%)
  starting transfers between devices  45.4 us (28%)
  waiting for transfers between devices  35.8 us (22%)
  local copies, waits for them, and re-layouts  12.4 us (8%)
    pallas_call x2, Pallas kernels, conv_chunk(): pl.pallas_call(functools.partial(conv_kernel, first, frames), out_shape=o...  25.7 us
    pallas_call x2, Pallas kernels, frame_attention(): pl.pallas_call(frame_kernel, out_shape=jax.ShapeDtypeStruct((tokens, c),...  20.7 us
    all_to_all x2, waiting for transfers between devices, shards(): lax.all_to_all(out, ('rows', 'tm'), 0, 0, tiled=True)  19.2 us
    all_to_all x2, starting transfers between devices, shards(): lax.all_to_all(out, ('rows', 'tm'), 0, 0, tiled=True)  11.9 us
    pallas_call x1, Pallas kernels, time_finish(): pl.pallas_call(time_kernel, out_shape=jax.ShapeDtypeStruct((16, 128, c),...  11.3 us
    ppermute x2, waiting for transfers between devices, shards(): lax.ppermute(top[k:k + half], 'rows', down)  11 us
    all_to_all x2, starting transfers between devices, shards(): lax.all_to_all(conv, 'rows', 0, 0, tiled=True)  10 us
    ppermute x2, starting transfers between devices, shards(): lax.ppermute(bottom[k:k + half], 'rows', up)  7.24 us
  transfers between devices with their start and end apart: 11, of which 5 were waited for; matrix products, arithmetic and copies ran while one was open for 4% of the time, Pallas kernels for 25%

profile of v1, /device:TPU:1, one launch (start us, length us, event | category | flops | bytes accessed | tf_op | source)
XLA Modules:
  0.0 159.2 jit_solution(8621177515220209906)
XLA Ops:
  0.0 0.0 copy-start
  0.0 1.0 slice_bitcast_fusion.4
  1.0 4.9 %collective-permute-start.6 = (bf16[2,32,512]{2,1,0:T(8,128)(2,1)S(1)}, bf16[2,32,512]{2,1,0:T(8,128)(2,1)S(1)}, u32[]{:S(2)}, u32[]{:S(2)}) collective-permute-start(bf16[2,32,512]{2,1,0:T(8,128)(2,1)S(1)} %get-tuple-element.19), channel_id=1, source_target_pairs={{1,8},{2,9},{3,10},{4,11},{5,12},{6,13},{7,14},{9,16},{10,17},{11,... | collective-permute-start | bytes 196616 | tf_op jit(solution)/shard_map/ppermute | solution.py:332
  6.0 4.2 %collective-permute-start.5 = (bf16[2,32,512]{2,1,0:T(8,128)(2,1)S(1)}, bf16[2,32,512]{2,1,0:T(8,128)(2,1)S(1)}, u32[]{:S(2)}, u32[]{:S(2)}) collective-permute-start(bf16[2,32,512]{2,1,0:T(8,128)(2,1)S(1)} %get-tuple-element.20), channel_id=1, source_target_pairs={{0,9},{1,10},{2,11},{3,12},{4,13},{5,14},{6,15},{8,17},{9,18},{10,... | collective-permute-start | bytes 196616 | tf_op jit(solution)/shard_map/ppermute | solution.py:331
  10.2 1.0 slice.92
  11.1 3.3 %collective-permute-start.4 = (bf16[2,4,32,512]{3,2,1,0:T(8,128)(2,1)S(1)}, bf16[2,4,32,512]{3,2,1,0:T(8,128)(2,1)S(1)}, u32[]{:S(2)}, u32[]{:S(2)}) collective-permute-start(bf16[2,4,32,512]{3,2,1,0:T(8,128)(2,1)S(1)} %slice.92), channel_id=1, source_target_pairs={{0,8},{8,16},{16,24},{24,32},{32,40},{40,48},{48,56},{56,64},{64,7... | collective-permute-start | bytes 786440 | tf_op jit(solution)/shard_map/ppermute | solution.py:329
  14.4 1.3 slice_bitcast_fusion
  15.7 2.0 %collective-permute-start.3 = (bf16[8,32,512]{2,1,0:T(8,128)(2,1)S(1)}, bf16[8,32,512]{2,1,0:T(8,128)(2,1)S(1)}, u32[]{:S(2)}, u32[]{:S(2)}) collective-permute-start(bf16[8,32,512]{2,1,0:T(8,128)(2,1)S(1)} %get-tuple-element.21), channel_id=1, source_target_pairs={{1,0},{2,1},{3,2},{4,3},{5,4},{6,5},{7,6},{9,8},{10,9},{11,10},{12... | collective-permute-start | bytes 786440 | tf_op jit(solution)/shard_map/ppermute | solution.py:326
  17.7 3.6 %collective-permute-start.2 = (bf16[8,32,512]{2,1,0:T(8,128)(2,1)S(1)}, bf16[8,32,512]{2,1,0:T(8,128)(2,1)S(1)}, u32[]{:S(2)}, u32[]{:S(2)}) collective-permute-start(bf16[8,32,512]{2,1,0:T(8,128)(2,1)S(1)} %get-tuple-element.22), channel_id=1, source_target_pairs={{0,1},{1,2},{2,3},{3,4},{4,5},{5,6},{6,7},{8,9},{9,10},{10,11},{11... | collective-permute-start | bytes 786440 | tf_op jit(solution)/shard_map/ppermute | solution.py:326
  21.3 0.0 copy-done
  21.3 0.0 copy-start.6
  21.3 1.6 fusion.1
  22.9 0.0 copy-done.6
  22.9 0.1 pad_dynamic-slice_fusion
  22.9 0.1 fusion
  23.0 0.6 fusion.2
  23.6 0.0 collective-permute-done.6.refs_5_
  23.6 0.0 copy-start.12
  23.6 0.0 collective-permute-done.5.refs_4_
  23.7 0.0 copy-start.13
  23.7 0.0 collective-permute-done.4
  23.7 0.0 copy-start.7
  23.7 0.0 collective-permute-done.3.refs_2_
  23.7 0.0 copy-start.8
  23.7 0.9 collective-permute-done.2.refs_1_
  24.6 0.0 copy-start.9
  24.6 0.0 copy-done.12
  24.6 0.0 copy-done.13
  24.6 0.0 copy-done.7
  24.6 0.0 copy-done.8
  24.6 0.7 copy-done.9
  25.3 13.6 %conv_chunk.2 = (bf16[8,128,512]{2,1,0:T(8,128)(2,1)}, bf16[2,128,512]{2,1,0:T(8,128)(2,1)}) custom-call(s32[2,8]{1,0:T(2,128)} %get-tuple-element.27.idx_ref, bf16[8,128,512]{2,1,0:T(8,128)(2,1)} %bitcast.47, bf16[8,32,512]{2,1,0:T(8,128)(2,1)} %copy-done.9, bf16[8,32,512]{2,1,0:T(8,128)(2,1)} %copy-done.8, bf16[2,128,512]{2,1,0:T(8,128)(2,1)} %bitcast.52, ...), custom_call_target="tpu_custom_call" | custom-call | flops 7650410496 | bytes 9437184 | tf_op jit(solution)/shard_map/conv_chunk/pallas_call | solution.py:123
  38.9 5.9 %all-to-all-start.2 = ((bf16[8,128,512]{2,1,0:T(8,128)(2,1)}), bf16[8,128,512]{2,1,0:T(8,128)(2,1)S(1)}, u32[]{:S(2)}, u32[]{:S(2)}) async-start(bf16[8,128,512]{2,1,0:T(8,128)(2,1)} %get-tuple-element.12), calls=%async_computation.2 | async-start | bytes 2097152 | tf_op jit(solution)/shard_map/all_to_all | solution.py:349
  44.7 1.9 %collective-permute-start.1 = (bf16[8,32,512]{2,1,0:T(8,128)(2,1)S(1)}, bf16[8,32,512]{2,1,0:T(8,128)(2,1)S(1)}, u32[]{:S(2)}, u32[]{:S(2)}) collective-permute-start(bf16[8,32,512]{2,1,0:T(8,128)(2,1)S(1)} %get-tuple-element.23), channel_id=1, source_target_pairs={{1,0},{2,1},{3,2},{4,3},{5,4},{6,5},{7,6},{9,8},{10,9},{11,10},{12... | collective-permute-start | bytes 786440 | tf_op jit(solution)/shard_map/ppermute | solution.py:326
  46.7 3.6 %collective-permute-start = (bf16[8,32,512]{2,1,0:T(8,128)(2,1)S(1)}, bf16[8,32,512]{2,1,0:T(8,128)(2,1)S(1)}, u32[]{:S(2)}, u32[]{:S(2)}) collective-permute-start(bf16[8,32,512]{2,1,0:T(8,128)(2,1)S(1)} %get-tuple-element.24), channel_id=1, source_target_pairs={{0,1},{1,2},{2,3},{3,4},{4,5},{5,6},{6,7},{8,9},{9,10},{10,11},{11... | collective-permute-start | bytes 786440 | tf_op jit(solution)/shard_map/ppermute | solution.py:326
  50.3 11.0 %collective-permute-done.1.refs_2_ = bf16[8,32,512]{2,1,0:T(8,128)(2,1)S(1)} collective-permute-done((bf16[8,32,512]{2,1,0:T(8,128)(2,1)S(1)}, bf16[8,32,512]{2,1,0:T(8,128)(2,1)S(1)}, u32[]{:S(2)}, u32[]{:S(2)}) %collective-permute-start.1) | collective-permute-done | bytes 262176 | tf_op jit(solution)/shard_map/ppermute | solution.py:326
  61.3 0.0 copy-start.10
  61.3 0.0 collective-permute-done.refs_1_
  61.3 0.0 copy-start.11
  61.3 0.7 copy-done.10
  62.0 0.1 copy-done.11
  62.1 12.1 %conv_chunk.3 = bf16[8,128,512]{2,1,0:T(8,128)(2,1)} custom-call(s32[2,8]{1,0:T(2,128)} %get-tuple-element.28.idx_ref, bf16[8,128,512]{2,1,0:T(8,128)(2,1)} %bitcast.46, bf16[8,32,512]{2,1,0:T(8,128)(2,1)} %copy-done.11, bf16[8,32,512]{2,1,0:T(8,128)(2,1)} %copy-done.10, bf16[2,128,512]{2,1,0:T(8,128)(2,1)} %get-tuple-element.11.refs_3_, ...), custom_call_target="tpu_custom_call" | custom-call | flops 6442450944 | bytes 9437184 | tf_op jit(solution)/shard_map/conv_chunk/pallas_call | solution.py:123
  74.3 0.0 all-to-all-done.2
  74.3 0.0 copy-start.1
  74.3 4.1 %all-to-all-start = ((bf16[8,128,512]{2,1,0:T(8,128)(2,1)}), bf16[8,128,512]{2,1,0:T(8,128)(2,1)S(1)}, u32[]{:S(2)}, u32[]{:S(2)}) async-start(bf16[8,128,512]{2,1,0:T(8,128)(2,1)} %conv_chunk.3), calls=%async_computation | async-start | bytes 2097152 | tf_op jit(solution)/shard_map/all_to_all | solution.py:349
  78.4 0.0 copy-done.1
  78.4 10.4 %frame_attention.3 = bf16[1024,512]{1,0:T(8,128)(2,1)} custom-call(bf16[1024,512]{1,0:T(8,128)(2,1)} %bitcast.38, bf16[1024,512]{1,0:T(8,128)(2,1)} %bitcast.39, bf16[4,512,512]{2,1,0:T(8,128)(2,1)} %w_ref.5), custom_call_target="tpu_custom_call" | custom-call | flops 4294967296 | bytes 5242880 | tf_op jit(solution)/shard_map/frame_attention/pallas_call | solution.py:190
  88.8 4.7 %all-to-all-done = bf16[8,128,512]{2,1,0:T(8,128)(2,1)S(1)} async-done(((bf16[8,128,512]{2,1,0:T(8,128)(2,1)}), bf16[8,128,512]{2,1,0:T(8,128)(2,1)S(1)}, u32[]{:S(2)}, u32[]{:S(2)}) %all-to-all-start) | async-done | bytes 1048608 | tf_op jit(solution)/shard_map/all_to_all | solution.py:349
  93.5 0.0 copy-start.4
  93.5 7.0 %all-to-all-start.3 = ((bf16[128,8,512]{2,1,0:T(8,128)(2,1)}), bf16[128,8,512]{2,1,0:T(8,128)(2,1)S(1)}, u32[]{:S(2)}, u32[]{:S(2)}) async-start(bf16[128,8,512]{2,1,0:T(8,128)(2,1)} %bitcast.45), calls=%async_computation.3 | async-start | bytes 2097152 | tf_op jit(solution)/shard_map/all_to_all | solution.py:352
  100.5 0.0 copy-done.4
  100.5 10.4 %frame_attention.2 = bf16[1024,512]{1,0:T(8,128)(2,1)} custom-call(bf16[1024,512]{1,0:T(8,128)(2,1)} %bitcast.43, bf16[1024,512]{1,0:T(8,128)(2,1)} %bitcast.44, bf16[4,512,512]{2,1,0:T(8,128)(2,1)} %w_ref.5), custom_call_target="tpu_custom_call" | custom-call | flops 4294967296 | bytes 5242880 | tf_op jit(solution)/shard_map/frame_attention/pallas_call | solution.py:190
  110.9 8.2 %all-to-all-done.3 = bf16[128,8,512]{2,1,0:T(8,128)(2,1)S(1)} async-done(((bf16[128,8,512]{2,1,0:T(8,128)(2,1)}), bf16[128,8,512]{2,1,0:T(8,128)(2,1)S(1)}, u32[]{:S(2)}, u32[]{:S(2)}) %all-to-all-start.3) | async-done | bytes 1048608 | tf_op jit(solution)/shard_map/all_to_all | solution.py:352
  119.2 4.9 %all-to-all-start.1 = ((bf16[128,8,512]{2,1,0:T(8,128)(2,1)}), bf16[128,8,512]{2,1,0:T(8,128)(2,1)S(1)}, u32[]{:S(2)}, u32[]{:S(2)}) async-start(bf16[128,8,512]{2,1,0:T(8,128)(2,1)} %bitcast.41), calls=%async_computation.1 | async-start | bytes 2097152 | tf_op jit(solution)/shard_map/all_to_all | solution.py:352
  124.1 0.1 reshape.48
  124.2 0.1 eq.25
  124.3 0.0 copy-done.5
  124.3 0.8 and_select_fusion.bias_ref
  125.1 0.0 copy-done.2
  125.1 6.8 %time_qkv.1 = (bf16[8,128,512]{2,1,0:T(8,128)(2,1)}, bf16[8,128,512]{2,1,0:T(8,128)(2,1)}, bf16[8,128,512]{2,1,0:T(8,128)(2,1)}, bf16[8,128,512]{2,1,0:T(8,128)(2,1)}) custom-call(bf16[8,128,512]{2,1,0:T(8,128)(2,1)} %bitcast.40, bf16[4,512,512]{2,1,0:T(8,128)(2,1)} %w_ref.7), custom_call_target="tpu_custom_call" | custom-call | flops 1610612736 | bytes 7340032 | tf_op jit(solution)/shard_map/time_qkv/pallas_call | solution.py:247
  131.9 10.9 %all-to-all-done.1 = bf16[128,8,512]{2,1,0:T(8,128)(2,1)S(1)} async-done(((bf16[128,8,512]{2,1,0:T(8,128)(2,1)}), bf16[128,8,512]{2,1,0:T(8,128)(2,1)S(1)}, u32[]{:S(2)}, u32[]{:S(2)}) %all-to-all-start.1) | async-done | bytes 1048608 | tf_op jit(solution)/shard_map/all_to_all | solution.py:352
  142.8 1.0 copy-done.3
  143.8 11.3 %time_finish.1 = bf16[16,128,512]{2,1,0:T(8,128)(2,1)} custom-call(bf16[8,128,512]{2,1,0:T(8,128)(2,1)} %bitcast.42, f32[256,256]{1,0:T(8,128)} %and_select_fusion.bias_ref, bf16[4,512,512]{2,1,0:T(8,128)(2,1)} %w_ref.7, bf16[8,128,512]{2,1,0:T(8,128)(2,1)} %get-tuple-element.13.x0_hbm, bf16[8,128,512]{2,1,0:T(8,128)(2,1)} %get-tuple-element.14.q0_hbm, ...), custom_call_target="tpu_custom_call" | custom-call | flops 3758096384 | bytes 10485760 | tf_op jit(solution)/shard_map/time_finish/pallas_call | solution.py:296
  155.1 4.1 %reshape.51 = bf16[256,4,2,512]{3,2,1,0:T(2,128)(2,1)} reshape(bf16[16,128,512]{2,1,0:T(8,128)(2,1)} %time_finish.1) | data formatting | bytes 4194304 | tf_op jit(solution)/shard_map/reshape | solution.py:363
  (5 shorter events, 0.0 us)
Async XLA Ops:
  0.0 21.3 %copy-start = (bf16[16,4,32,512]{3,2,1,0:T(8,128)(2,1)S(1)}, bf16[16,4,32,512]{3,2,1,0:T(8,128)(2,1)}, u32[]{:S(2)}) copy-start(bf16[16,4,32,512]{3,2,1,0:T(8,128)(2,1)} %param.7) | copy-start | bytes 6291460
  1.0 22.6 %collective-permute-start.6 = (bf16[2,32,512]{2,1,0:T(8,128)(2,1)S(1)}, bf16[2,32,512]{2,1,0:T(8,128)(2,1)S(1)}, u32[]{:S(2)}, u32[]{:S(2)}) collective-permute-start(bf16[2,32,512]{2,1,0:T(8,128)(2,1)S(1)} %get-tuple-element.19), channel_id=1, source_target_pairs={{1,8},{2,9},{3,10},{4,11},{5,12},{6,13},{7,14},{9,16},{10,17},{11,... | collective-permute-start | bytes 196616 | tf_op jit(solution)/shard_map/ppermute | solution.py:332
  6.0 17.7 %collective-permute-start.5 = (bf16[2,32,512]{2,1,0:T(8,128)(2,1)S(1)}, bf16[2,32,512]{2,1,0:T(8,128)(2,1)S(1)}, u32[]{:S(2)}, u32[]{:S(2)}) collective-permute-start(bf16[2,32,512]{2,1,0:T(8,128)(2,1)S(1)} %get-tuple-element.20), channel_id=1, source_target_pairs={{0,9},{1,10},{2,11},{3,12},{4,13},{5,14},{6,15},{8,17},{9,18},{10,... | collective-permute-start | bytes 196616 | tf_op jit(solution)/shard_map/ppermute | solution.py:331
  11.1 12.5 %collective-permute-start.4 = (bf16[2,4,32,512]{3,2,1,0:T(8,128)(2,1)S(1)}, bf16[2,4,32,512]{3,2,1,0:T(8,128)(2,1)S(1)}, u32[]{:S(2)}, u32[]{:S(2)}) collective-permute-start(bf16[2,4,32,512]{3,2,1,0:T(8,128)(2,1)S(1)} %slice.92), channel_id=1, source_target_pairs={{0,8},{8,16},{16,24},{24,32},{32,40},{40,48},{48,56},{56,64},{64,7... | collective-permute-start | bytes 786440 | tf_op jit(solution)/shard_map/ppermute | solution.py:329
  15.7 8.0 %collective-permute-start.3 = (bf16[8,32,512]{2,1,0:T(8,128)(2,1)S(1)}, bf16[8,32,512]{2,1,0:T(8,128)(2,1)S(1)}, u32[]{:S(2)}, u32[]{:S(2)}) collective-permute-start(bf16[8,32,512]{2,1,0:T(8,128)(2,1)S(1)} %get-tuple-element.21), channel_id=1, source_target_pairs={{1,0},{2,1},{3,2},{4,3},{5,4},{6,5},{7,6},{9,8},{10,9},{11,10},{12... | collective-permute-start | bytes 786440 | tf_op jit(solution)/shard_map/ppermute | solution.py:326
  17.7 6.9 %collective-permute-start.2 = (bf16[8,32,512]{2,1,0:T(8,128)(2,1)S(1)}, bf16[8,32,512]{2,1,0:T(8,128)(2,1)S(1)}, u32[]{:S(2)}, u32[]{:S(2)}) collective-permute-start(bf16[8,32,512]{2,1,0:T(8,128)(2,1)S(1)} %get-tuple-element.22), channel_id=1, source_target_pairs={{0,1},{1,2},{2,3},{3,4},{4,5},{5,6},{6,7},{8,9},{9,10},{10,11},{11... | collective-permute-start | bytes 786440 | tf_op jit(solution)/shard_map/ppermute | solution.py:326
  21.3 1.6 copy-start.6
  23.6 0.9 copy-start.12
  23.7 0.9 copy-start.13
  23.7 0.9 copy-start.7
  23.7 0.9 copy-start.8
  24.6 0.7 copy-start.9
  38.9 35.4 %all-to-all-start.2 = ((bf16[8,128,512]{2,1,0:T(8,128)(2,1)}), bf16[8,128,512]{2,1,0:T(8,128)(2,1)S(1)}, u32[]{:S(2)}, u32[]{:S(2)}) async-start(bf16[8,128,512]{2,1,0:T(8,128)(2,1)} %get-tuple-element.12), calls=%async_computation.2 | async-start | bytes 2097152 | tf_op jit(solution)/shard_map/all_to_all | solution.py:349
  44.7 16.6 %collective-permute-start.1 = (bf16[8,32,512]{2,1,0:T(8,128)(2,1)S(1)}, bf16[8,32,512]{2,1,0:T(8,128)(2,1)S(1)}, u32[]{:S(2)}, u32[]{:S(2)}) collective-permute-start(bf16[8,32,512]{2,1,0:T(8,128)(2,1)S(1)} %get-tuple-element.23), channel_id=1, source_target_pairs={{1,0},{2,1},{3,2},{4,3},{5,4},{6,5},{7,6},{9,8},{10,9},{11,10},{12... | collective-permute-start | bytes 786440 | tf_op jit(solution)/shard_map/ppermute | solution.py:326
  46.7 14.7 %collective-permute-start = (bf16[8,32,512]{2,1,0:T(8,128)(2,1)S(1)}, bf16[8,32,512]{2,1,0:T(8,128)(2,1)S(1)}, u32[]{:S(2)}, u32[]{:S(2)}) collective-permute-start(bf16[8,32,512]{2,1,0:T(8,128)(2,1)S(1)} %get-tuple-element.24), channel_id=1, source_target_pairs={{0,1},{1,2},{2,3},{3,4},{4,5},{5,6},{6,7},{8,9},{9,10},{10,11},{11... | collective-permute-start | bytes 786440 | tf_op jit(solution)/shard_map/ppermute | solution.py:326
  61.3 0.7 copy-start.10
  61.3 0.8 copy-start.11
  74.3 4.1 %copy-start.1 = (bf16[8,128,512]{2,1,0:T(8,128)(2,1)}, bf16[8,128,512]{2,1,0:T(8,128)(2,1)S(1)}, u32[]{:S(2)}) copy-start(bf16[8,128,512]{2,1,0:T(8,128)(2,1)S(1)} %all-to-all-done.2) | copy-start | bytes 3145732
  74.3 19.2 %all-to-all-start = ((bf16[8,128,512]{2,1,0:T(8,128)(2,1)}), bf16[8,128,512]{2,1,0:T(8,128)(2,1)S(1)}, u32[]{:S(2)}, u32[]{:S(2)}) async-start(bf16[8,128,512]{2,1,0:T(8,128)(2,1)} %conv_chunk.3), calls=%async_computation | async-start | bytes 2097152 | tf_op jit(solution)/shard_map/all_to_all | solution.py:349
  93.5 7.0 %copy-start.4 = (bf16[8,128,512]{2,1,0:T(8,128)(2,1)}, bf16[8,128,512]{2,1,0:T(8,128)(2,1)S(1)}, u32[]{:S(2)}) copy-start(bf16[8,128,512]{2,1,0:T(8,128)(2,1)S(1)} %all-to-all-done) | copy-start | bytes 3145732
  93.5 25.6 %all-to-all-start.3 = ((bf16[128,8,512]{2,1,0:T(8,128)(2,1)}), bf16[128,8,512]{2,1,0:T(8,128)(2,1)S(1)}, u32[]{:S(2)}, u32[]{:S(2)}) async-start(bf16[128,8,512]{2,1,0:T(8,128)(2,1)} %bitcast.45), calls=%async_computation.3 | async-start | bytes 2097152 | tf_op jit(solution)/shard_map/all_to_all | solution.py:352
  110.9 13.4 %copy-start.5 = (s32[256]{0:T(256)S(1)}, s32[256]{0:T(256)}, u32[]{:S(2)}) copy-start(s32[256]{0:T(256)} %constant.39.clone) | copy-start | bytes 3076
  119.1 6.0 %copy-start.2 = (bf16[128,8,512]{2,1,0:T(8,128)(2,1)}, bf16[128,8,512]{2,1,0:T(8,128)(2,1)S(1)}, u32[]{:S(2)}) copy-start(bf16[128,8,512]{2,1,0:T(8,128)(2,1)S(1)} %all-to-all-done.3) | copy-start | bytes 3145732
  119.2 23.7 %all-to-all-start.1 = ((bf16[128,8,512]{2,1,0:T(8,128)(2,1)}), bf16[128,8,512]{2,1,0:T(8,128)(2,1)S(1)}, u32[]{:S(2)}, u32[]{:S(2)}) async-start(bf16[128,8,512]{2,1,0:T(8,128)(2,1)} %bitcast.41), calls=%async_computation.1 | async-start | bytes 2097152 | tf_op jit(solution)/shard_map/all_to_all | solution.py:352
  142.8 1.0 copy-start.3

commit v2 on v0

v2 whole, which is shorter than its diff:
```python
import functools

import jax
import jax.numpy as jnp
from jax import lax
from jax.experimental import pallas as pl
from jax.experimental.pallas import tpu as pltpu
from jax.sharding import PartitionSpec as P

GROUPS = 32
EPS = 1e-06
MASKED = -1e30
LOG2E = 1.4426950408889634
BF = jnp.bfloat16
F32 = jnp.float32
VMEM_LIMIT = 16 * 1024 * 1024


def mm(a, b):
    return jnp.dot(a, b, preferred_element_type=F32)


def mm_nt(a, b):
    return lax.dot_general(a, b, (((1,), (1,)), ((), ())), preferred_element_type=F32)


def one_hot_rows(n, source_of):
    out_row = lax.broadcasted_iota(jnp.int32, (n, n), 0)
    in_row = lax.broadcasted_iota(jnp.int32, (n, n), 1)
    return jnp.where(in_row == source_of(out_row), 1.0, 0.0).astype(BF)


def space_taps(blocks, rows, lhs_of, w_ref, acc, store):
    c = acc.shape[-1]
    row = lax.broadcasted_iota(jnp.int32, (rows, c), 0) & 31

    def product(block, col):
        weights = jnp.concatenate([w_ref[3 * a + col] for a in range(3)], axis=0)
        return mm(lhs_of(block), weights)

    def span(block):
        return slice(block * rows, (block + 1) * rows)

    for block in range(blocks):
        acc[span(block)] = jnp.where(row == 0, 0.0, pltpu.roll(product(block, 0), 1, 0))
    for block in range(blocks):
        acc[span(block)] += product(block, 1)
    for block in range(blocks):
        v = acc[span(block)] + jnp.where(row == 31, 0.0, pltpu.roll(product(block, 2), rows - 1, 0))
        half = 0.5 * v
        store(block, (half + half * jnp.tanh(half)).astype(BF))


def inner_kernel(x_ref, w_ref, out_ref, acc):
    frames, tokens, c = out_ref.shape
    per = 8

    def lhs_of(block):
        f = slice(block * per, (block + 1) * per)
        return jnp.concatenate(
            [x_ref[f, 32 * a : 32 * a + tokens, :].reshape(per * tokens, c) for a in range(3)], axis=1
        )

    def store(block, hidden):
        out_ref[block * per : (block + 1) * per] = hidden.reshape(per, tokens, c)

    space_taps(frames // per, per * tokens, lhs_of, w_ref, acc, store)


def conv_inner(x, w_space):
    frames, tokens, c = x.shape
    rows = frames * (tokens - 64)
    vmem = pl.BlockSpec(memory_space=pltpu.VMEM)
    return pl.pallas_call(
        inner_kernel,
        out_shape=jax.ShapeDtypeStruct((frames, tokens - 64, c), BF),
        in_specs=[vmem] * 2,
        out_specs=vmem,
        scratch_shapes=[pltpu.VMEM((rows, c), F32)],
        compiler_params=pltpu.CompilerParams(vmem_limit_bytes=VMEM_LIMIT),
        cost_estimate=pl.CostEstimate(flops=18 * rows * c * c, bytes_accessed=8 * 2**20, transcendentals=0),
        name="conv_inner",
    )(x, w_space)


def outer_kernel(late, idx_ref, x_ref, up_ref, dn_ref, inner_ref, *refs):
    tokens, c = x_ref.shape[1:]
    count = 10 if late else 6
    frames = slice(6, 16) if late else slice(0, 6)
    if late:
        (w_ref, wt_ref, *outs, lead_ref, tail_ref, acc, hs) = refs
        here = slice(0, 10)
    else:
        (lead_ref, tail_ref, w_ref, wt_ref, *outs, acc, hs) = refs
        here = slice(2, 8)
    rows = count * 64

    hs[here, 32:96, :] = inner_ref[frames]
    if not late:
        hs[0:2] = tail_ref[...]
        hs[8:10] = lead_ref[...]

    def lhs_of(block):
        first = [up_ref[frames], x_ref[frames, 0:32, :], x_ref[frames, 32:64, :]]
        last = [x_ref[frames, 64:96, :], x_ref[frames, 96:128, :], dn_ref[frames]]
        return jnp.concatenate(
            [jnp.concatenate([f, l], axis=0).reshape(rows, c) for f, l in zip(first, last)], axis=1
        )

    def store(block, hidden):
        hidden = hidden.reshape(2, count, 32, c)
        hs[here, 0:32, :] = hidden[0]
        hs[here, 96:128, :] = hidden[1]

    space_taps(1, rows, lhs_of, w_ref, acc, store)

    order = one_hot_rows(128, lambda o: ((o >> 1) & 3) * 32 + (o >> 3) * 2 + (o & 1))
    weights = wt_ref[...].reshape(3 * c, c)
    per = 4
    for s0 in range(0, 8, per):
        taps = [jnp.concatenate([hs[idx_ref[k, s0 + s]] for s in range(per)], axis=0) for k in range(3)]
        y = mm(jnp.concatenate(taps, axis=1), weights)
        for s in range(per):
            own = y[s * tokens : (s + 1) * tokens] + x_ref[idx_ref[3, s0 + s]].astype(F32)
            outs[s0 + s][...] = mm(order, own.astype(BF)).astype(BF)
    if late:
        lead_ref[...] = hs[0:2]
        tail_ref[...] = hs[8:10]


def conv_outer(late, idx, x, up, dn, inner, given, w_space, w_time):
    tokens, c = x.shape[1:]
    count = 10 if late else 6
    ins = [x, up, dn, inner, *given, w_space, w_time]
    vmem = pl.BlockSpec(memory_space=pltpu.VMEM)
    out_shape = [jax.ShapeDtypeStruct((tokens, c), BF)] * 8
    if late:
        out_shape = out_shape + [jax.ShapeDtypeStruct((2, tokens, c), BF)] * 2
    rows = count * 64
    return pl.pallas_call(
        functools.partial(outer_kernel, late),
        out_shape=out_shape,
        in_specs=[pl.BlockSpec(memory_space=pltpu.SMEM)] + [vmem] * len(ins),
        out_specs=[vmem] * len(out_shape),
        scratch_shapes=[pltpu.VMEM((rows, c), F32), pltpu.VMEM((10, tokens, c), BF)],
        compiler_params=pltpu.CompilerParams(vmem_limit_bytes=VMEM_LIMIT),
        cost_estimate=pl.CostEstimate(
            flops=18 * rows * c * c + 48 * tokens * c * c, bytes_accessed=9 * 2**20, transcendentals=0
        ),
        name="conv_outer",
    )(idx, *ins)


def softmax_rows(scores, scale):
    top = jnp.max(scores, axis=-1, keepdims=True)
    raised = jnp.exp2((scores - top) * scale)
    return (raised * (1.0 / jnp.sum(raised, axis=-1, keepdims=True))).astype(BF)


def group_sum(v, per_group):
    lane = lax.broadcasted_iota(jnp.int32, v.shape, 1)
    n = v.shape[1]
    d = 1
    while d < per_group:
        v = v + jnp.where((lane & d) == 0, pltpu.roll(v, n - d, 1), pltpu.roll(v, d, 1))
        d *= 2
    return v


def frame_kernel(pair, place_ref, *refs):
    xs, (w_ref, other_ref, out_ref, q_s, k_s, v_s) = refs[:8], refs[8:]
    block, c = xs[0].shape
    tokens = 8 * block
    per_group = c // GROUPS
    entries = tokens * per_group

    sums, squares = 0.0, 0.0
    for ref in xs:
        values = ref[...].astype(F32)
        sums = sums + jnp.sum(values, axis=0, keepdims=True)
        squares = squares + jnp.sum(values * values, axis=0, keepdims=True)
    both = group_sum(jnp.concatenate([sums, squares] * 4, axis=0), per_group) / entries
    average, square = both[0:1], both[1:2]
    inverse = lax.rsqrt(square - average * average + EPS)
    for s in range(0, 8, 2):
        values = jnp.concatenate([xs[s][...], xs[s + 1][...]], axis=0).astype(F32)
        normed = ((values - average) * inverse).astype(BF)
        for i, ref in enumerate((q_s, k_s, v_s)):
            ref[s * block : (s + 2) * block] = mm(normed, w_ref[i]).astype(BF)
    for s in range(0, 8, 2):
        q = q_s[s * block : (s + 2) * block]
        probs = softmax_rows(mm_nt(q, k_s[...]), c ** (-0.5) * LOG2E)
        y = mm(mm(probs, v_s[...]).astype(BF), w_ref[3])
        for k in range(2):
            part = y[k * block : (k + 1) * block] + xs[s + k][...].astype(F32)
            if pair:
                other = other_ref[place_ref[s + k]].astype(F32).reshape(block // 8, 8, c)
                part = jnp.concatenate([part.reshape(block // 8, 8, c), other], axis=1)
            out_ref[place_ref[s + k]] = part.reshape(-1, c).astype(BF)


def frame_attention(pair, place, xs, weights, other):
    block, c = xs[0].shape
    tokens = 8 * block
    vmem = pl.BlockSpec(memory_space=pltpu.VMEM)
    return pl.pallas_call(
        functools.partial(frame_kernel, pair),
        out_shape=jax.ShapeDtypeStruct((8, block * (2 if pair else 1), c), BF),
        in_specs=[pl.BlockSpec(memory_space=pltpu.SMEM)]
        + [vmem] * 9
        + [vmem if pair else pl.BlockSpec(memory_space=pl.ANY)],
        out_specs=vmem,
        scratch_shapes=[pltpu.VMEM((tokens, c), BF)] * 3,
        compiler_params=pltpu.CompilerParams(vmem_limit_bytes=VMEM_LIMIT),
        cost_estimate=pl.CostEstimate(
            flops=8 * tokens * c * c + 4 * tokens * tokens * c,
            bytes_accessed=4 * 2**20,
            transcendentals=tokens * tokens,
        ),
        name="frame_attention",
    )(place, *xs, weights, other)


def by_cell(o):
    return (o & 7) * 32 + ((o >> 3) & 3) * 8 + (o >> 5)


def by_frame(o):
    return (o & 7) * 32 + (o >> 3)


def project_time(x, w_ref):
    values = x.astype(F32)
    average = jnp.mean(values, axis=-1, keepdims=True)
    centered = values - average
    spread = jnp.mean(centered * centered, axis=-1, keepdims=True)
    normed = (centered * lax.rsqrt(spread + EPS)).astype(BF)
    return [mm(normed, w_ref[i]).astype(BF) for i in range(3)]


def time_kernel(x_ref, bias_ref, w_ref, out_ref, x_s, q_s, k_s, v_s):
    c = x_ref.shape[-1]
    order = one_hot_rows(256, by_cell)
    for u in range(8):
        span = slice(32 * u, 32 * u + 32)
        x = mm(order, x_ref[:, span, :].reshape(256, c)).astype(BF)
        for ref, value in zip((x_s, q_s, k_s, v_s), [x, *project_time(x, w_ref)]):
            ref[:, span, :] = value.reshape(8, 32, c)
    for cell in range(8):
        scores = mm_nt(q_s[cell], k_s[cell]) * (c ** (-0.5) * LOG2E) + bias_ref[...]
        q_s[cell] = mm(softmax_rows(scores, 1.0), v_s[cell]).astype(BF)
    back = one_hot_rows(256, by_frame)
    for u in range(8):
        span = slice(32 * u, 32 * u + 32)
        y = mm(q_s[:, span, :].reshape(256, c), w_ref[3])
        y = (y + x_s[:, span, :].reshape(256, c).astype(F32)).astype(BF)
        out_ref[span] = mm(back, y).astype(BF).reshape(32, 4, 2, c)


def time_attention(x, bias, weights):
    r, tc, c = x.shape
    vmem = pl.BlockSpec(memory_space=pltpu.VMEM)
    return pl.pallas_call(
        time_kernel,
        out_shape=jax.ShapeDtypeStruct((256, 4, 2, c), BF),
        in_specs=[vmem] * 3,
        out_specs=vmem,
        scratch_shapes=[pltpu.VMEM((8, 256, c), BF)] * 4,
        compiler_params=pltpu.CompilerParams(vmem_limit_bytes=24 * 2**20),
        cost_estimate=pl.CostEstimate(
            flops=8 * r * tc * c * c + 8 * 4 * 256 * 256 * c,
            bytes_accessed=6 * 2**20,
            transcendentals=8 * 256 * 256,
        ),
        name="time_attention",
    )(x, bias, weights)


def shards(video, video_ids, w_space, w_time, spatial_attn, time_attn):
    frames, rows, cols, c = video.shape
    tm_count, rows_count = lax.axis_size("tm"), lax.axis_size("rows")
    half = frames // 2
    tokens = rows * cols
    me = lax.axis_index("rows")
    around = lambda a, by: lax.ppermute(
        a, "rows", [(i, (i + by) % rows_count) for i in range(rows_count)]
    )

    up = lax.ppermute(video[:, rows - 1], "rows", [(i, i + 1) for i in range(rows_count - 1)])
    dn = lax.ppermute(video[:, 0], "rows", [(i + 1, i) for i in range(rows_count - 1)])
    x = video.reshape(frames, tokens, c)
    inner = conv_inner(x, w_space)

    ids = jnp.concatenate([jnp.full((2,), -1, jnp.int32), video_ids])
    ids = lax.dynamic_slice_in_dim(ids, lax.axis_index("tm") * frames, frames + 2)
    place = jnp.arange(frames, dtype=jnp.int32) % half
    one = jnp.where(ids[1:-1] == ids[2:], place + 1, place + 2)
    two = jnp.where(ids[:-2] == ids[2:], place, one)

    def slots(late):
        own = slice(half, frames) if late else slice(0, half)
        first = half if late else 0
        table = jnp.stack([place[own] + 2, one[own], two[own], place[own] + first])
        return lax.dynamic_slice_in_dim(jnp.concatenate([table, table], axis=1), me, half, axis=1)

    *late, lead, tail = conv_outer(True, slots(True), x, up, dn, inner, [], w_space, w_time)
    tail = lax.ppermute(tail, "tm", [(t, t + 1) for t in range(tm_count - 1)])
    early = conv_outer(False, slots(False), x, up, dn, inner, [lead, tail], w_space, w_time)

    sources = lax.rem(me - jnp.arange(rows_count, dtype=jnp.int32) + rows_count, rows_count)
    def exchanged(conv):
        return [conv[0]] + [around(conv[s], s) for s in range(1, rows_count)]

    done = frame_attention(False, sources, exchanged(late), spatial_attn, early[0])
    done = frame_attention(True, sources, exchanged(early), spatial_attn, done)
    arrived = lax.all_to_all(
        done.reshape(rows_count * tm_count, -1, c), ("rows", "tm"), 0, 0, tiled=True
    ).reshape(rows_count, -1, c)

    number = jnp.arange(frames * tm_count, dtype=jnp.int32)
    allowed = (number[None, :] <= number[:, None]) & (video_ids[None, :] == video_ids[:, None])
    return time_attention(arrived, jnp.where(allowed, 0.0, MASKED).astype(F32), time_attn)


def solution(mesh):
    in_specs = (P("tm", "rows", None, None), P(), P(), P(), P(), P())
    out_specs = P(None, "rows", "tm", None)
    return jax.shard_map(shards, mesh=mesh, in_specs=in_specs, out_specs=out_specs, check_vma=False)
```

time: 270 us -> 125 us (0.46); the launches traced: 266 us -> 125 us
  matrix products: 83.8 us -> 0 us
  blocking collectives: 66.6 us -> 0 us
  Pallas kernels: 0 us -> 44.4 us
  local copies, waits for them, and re-layouts: 43.4 us -> 6.78 us
  starting transfers between devices: 17 us -> 40.7 us
  other arithmetic: 19.6 us -> 0.42 us
    dot_general x21 -> x0, matrix products: 75.2 us -> none  [the longest x9 38.3 us: space_conv(): jnp.dot(window.reshape(-1, channel_width), weights[row_shift * 3 + col_sh...]
    all_to_all x2 -> x0, blocking collectives: 66.6 us -> none  [the longest x1 33.7 us: shards(): lax.all_to_all(frame_out, 'tm', split_axis=2, concat_axis=0, tiled=True)]
    pallas_call x0 -> x6, Pallas kernels: none -> 44.4 us  [the longest x2 15.8 us: frame_attention(): pl.pallas_call(functools.partial(frame_kernel, pair), out_shape=jax.Shape...]
    convert_element_type x6 -> x0, local copies, waits for them, and re-layouts: 21.9 us -> none  [the longest x3 16.7 us: time_attention(): values = column_block.astype(jnp.float32)]
    ppermute x3 -> x17, starting transfers between devices: 10.1 us -> 26.5 us  [the longest x14 16.5 us: shards(): lax.ppermute(a, 'rows', [(i, (i + by) % rows_count) for i in range(rows_c...]
    convert_element_type x6 -> x0, other arithmetic: 8.57 us -> none  [the longest x1 3.44 us: shards(): hidden = jax.nn.silu(space_conv(padded, w_space)).astype(jnp.bfloat16)]
    sub x1 -> x0, matrix products: 8.53 us -> none  [finish(): raised = jnp.exp(attention_logits - top)]
    slice x3 -> x0, local copies, waits for them, and re-layouts: 7.94 us -> none  [the longest x1 5.48 us: space_conv(): widened[:, row_shift:row_shift + row_count, col_shift:col_shift + col_cou...]
  transfers between devices with their start and end apart: 4 -> 18, of which waited for: 4 -> 4; matrix products, arithmetic and copies ran while one was open for 1% -> 1% of each run, Pallas kernels for 0% -> 14%
where the time goes in v2:
time: 125 us
  Pallas kernels  44.4 us (36%)
  starting transfers between devices  40.7 us (33%)
  waiting for transfers between devices  32.8 us (26%)
  local copies, waits for them, and re-layouts  6.78 us (5%)
    all_to_all x1, waiting for transfers between devices, shards(): lax.all_to_all(done.reshape(rows_count * tm_count, -1, c), ('rows', 'tm')...  29.5 us
    ppermute x14, starting transfers between devices, shards(): lax.ppermute(a, 'rows', [(i, (i + by) % rows_count) for i in range(rows_c...  16.5 us
    pallas_call x2, Pallas kernels, frame_attention(): pl.pallas_call(functools.partial(frame_kernel, pair), out_shape=jax.Shape...  15.8 us
    all_to_all x1, starting transfers between devices, shards(): lax.all_to_all(done.reshape(rows_count * tm_count, -1, c), ('rows', 'tm')...  14.2 us
    pallas_call x1, Pallas kernels, time_attention(): pl.pallas_call(time_kernel, out_shape=jax.ShapeDtypeStruct((256, 4, 2, c)...  12.2 us
    pallas_call x2, Pallas kernels, conv_outer(): pl.pallas_call(functools.partial(outer_kernel, late), out_shape=out_shape...  11 us
    pallas_call x1, Pallas kernels, conv_inner(): pl.pallas_call(inner_kernel, out_shape=jax.ShapeDtypeStruct((frames, toke...  5.36 us
    ppermute x1, starting transfers between devices, shards(): lax.ppermute(video[:, rows - 1], 'rows', [(i, i + 1) for i in range(rows_...  4.58 us
  transfers between devices with their start and end apart: 18, of which 4 were waited for; matrix products, arithmetic and copies ran while one was open for 1% of the time, Pallas kernels for 14%

profile of v2, /device:TPU:1, one launch (start us, length us, event | category | flops | bytes accessed | tf_op | source)
XLA Modules:
  0.0 125.2 jit_solution(10951256904370711467)
XLA Ops:
  0.0 0.0 copy-start
  0.0 0.0 copy-start.5
  0.0 2.5 %slice_bitcast_fusion = (bf16[16,32,512]{2,1,0:T(8,128)(2,1)}, bf16[16,32,512]{2,1,0:T(8,128)(2,1)}) fusion(bf16[16,4,32,512]{3,2,1,0:T(8,128)(2,1)} %param.6), kind=kLoop, calls=%fused_computation | loop fusion | bytes 2097152 | tf_op jit(solution)/shard_map/squeeze | solution.py:290
  2.5 4.6 %collective-permute-start = (bf16[16,32,512]{2,1,0:T(8,128)(2,1)}, bf16[16,32,512]{2,1,0:T(8,128)(2,1)S(1)}, u32[]{:S(2)}, u32[]{:S(2)}) collective-permute-start(bf16[16,32,512]{2,1,0:T(8,128)(2,1)} %get-tuple-element.44), channel_id=1, source_target_pairs={{0,1},{1,2},{2,3},{3,4},{4,5},{5,6},{6,7},{8,9},{9,10},{10,11},{11... | collective-permute-start | bytes 1572872 | tf_op jit(solution)/shard_map/ppermute | solution.py:289
  7.1 1.9 %collective-permute-start.1 = (bf16[16,32,512]{2,1,0:T(8,128)(2,1)}, bf16[16,32,512]{2,1,0:T(8,128)(2,1)S(1)}, u32[]{:S(2)}, u32[]{:S(2)}) collective-permute-start(bf16[16,32,512]{2,1,0:T(8,128)(2,1)} %get-tuple-element.43), channel_id=1, source_target_pairs={{1,0},{2,1},{3,2},{4,3},{5,4},{6,5},{7,6},{9,8},{10,9},{11,10},{12... | collective-permute-start | bytes 1572872 | tf_op jit(solution)/shard_map/ppermute | solution.py:290
  9.0 0.0 copy-done.5
  9.0 0.1 pad_dynamic-slice_fusion
  9.1 0.1 compare_select_fusion.2
  9.2 0.1 add_bitcast_fusion.1
  9.2 0.1 slice_bitcast_fusion.3
  9.3 0.1 slice_bitcast_fusion.2
  9.4 0.1 add_add_fusion.1
  9.5 0.1 constant_dynamic-slice_fusion.idx_ref
  9.5 0.0 copy-done
  9.5 2.3 %copy-done.1 = bf16[9,512,512]{2,1,0:T(8,128)(2,1)S(1)} copy-done((bf16[9,512,512]{2,1,0:T(8,128)(2,1)S(1)}, bf16[9,512,512]{2,1,0:T(8,128)(2,1)}, u32[]{:S(2)}) %copy-start.1) | copy-done | bytes 4718616
  11.9 0.0 copy-start.4
  11.9 5.4 %conv_inner.1.inner_ref = bf16[16,64,512]{2,1,0:T(8,128)(2,1)S(1)} custom-call(bf16[16,128,512]{2,1,0:T(8,128)(2,1)S(1)} %bitcast.28, bf16[9,512,512]{2,1,0:T(8,128)(2,1)S(1)} %copy-done.1), custom_call_target="tpu_custom_call" | custom-call | flops 4831838208 | bytes 8388608 | tf_op jit(solution)/shard_map/conv_inner/pallas_call | solution.py:74
  17.2 0.0 collective-permute-done.up_ref
  17.3 0.5 collective-permute-done.1.dn_ref
  17.8 0.0 copy-done.4
  17.8 6.1 %conv_outer.2 = (bf16[128,512]{1,0:T(8,128)(2,1)S(1)}, bf16[128,512]{1,0:T(8,128)(2,1)S(1)}, bf16[128,512]{1,0:T(8,128)(2,1)S(1)}, bf16[128,512]{1,0:T(8,128)(2,...) custom-call(s32[4,8]{1,0:T(4,128)S(1)} %constant_dynamic-slice_fusio, ...), custom_call_target="tpu_custom_call" | custom-call | flops 4630511616 | bytes 9437184 | tf_op jit(solution)/shard_map/conv_outer/pallas_call | solution.py:140
  23.9 3.6 %collective-permute-start.2 = (bf16[2,128,512]{2,1,0:T(8,128)(2,1)S(1)}, bf16[2,128,512]{2,1,0:T(8,128)(2,1)S(1)}, u32[]{:S(2)}, u32[]{:S(2)}) collective-permute-start(bf16[2,128,512]{2,1,0:T(8,128)(2,1)S(1)} %get-tuple-element.24), channel_id=1, source_target_pairs={{0,8},{8,16},{16,24},{24,32},{32,40},{40,48},{48,56},{56,64},{64,7... | collective-permute-start | bytes 786440 | tf_op jit(solution)/shard_map/ppermute | solution.py:307
  27.5 0.1 add_add_fusion
  27.6 0.1 constant_dynamic-slice_fusion.1.idx_ref
  27.6 1.5 %collective-permute-start.10 = (bf16[128,512]{1,0:T(8,128)(2,1)S(1)}, bf16[128,512]{1,0:T(8,128)(2,1)S(1)}, u32[]{:S(2)}, u32[]{:S(2)}) collective-permute-start(bf16[128,512]{1,0:T(8,128)(2,1)S(1)} %get-tuple-element.34), channel_id=1, source_target_pairs={{0,1},{1,2},{2,3},{3,4},{4,5},{5,6},{6,7},{7,0},{8,9},{9,10},{10,1... | collective-permute-start | bytes 393224 | tf_op jit(solution)/shard_map/ppermute | solution.py:285
  29.2 1.3 %collective-permute-start.11 = (bf16[128,512]{1,0:T(8,128)(2,1)S(1)}, bf16[128,512]{1,0:T(8,128)(2,1)S(1)}, u32[]{:S(2)}, u32[]{:S(2)}) collective-permute-start(bf16[128,512]{1,0:T(8,128)(2,1)S(1)} %get-tuple-element.35), channel_id=1, source_target_pairs={{0,2},{1,3},{2,4},{3,5},{4,6},{5,7},{6,0},{7,1},{8,10},{9,11},{10,... | collective-permute-start | bytes 393224 | tf_op jit(solution)/shard_map/ppermute | solution.py:285
  30.5 1.6 %collective-permute-start.12 = (bf16[128,512]{1,0:T(8,128)(2,1)S(1)}, bf16[128,512]{1,0:T(8,128)(2,1)S(1)}, u32[]{:S(2)}, u32[]{:S(2)}) collective-permute-start(bf16[128,512]{1,0:T(8,128)(2,1)S(1)} %get-tuple-element.36), channel_id=1, source_target_pairs={{0,3},{1,4},{2,5},{3,6},{4,7},{5,0},{6,1},{7,2},{8,11},{9,12},{10,... | collective-permute-start | bytes 393224 | tf_op jit(solution)/shard_map/ppermute | solution.py:285
  32.1 0.5 collective-permute-start.13
  32.6 0.0 collective-permute-done.2.refs_1_
  32.6 2.4 %collective-permute-start.14 = (bf16[128,512]{1,0:T(8,128)(2,1)S(1)}, bf16[128,512]{1,0:T(8,128)(2,1)S(1)}, u32[]{:S(2)}, u32[]{:S(2)}) collective-permute-start(bf16[128,512]{1,0:T(8,128)(2,1)S(1)} %get-tuple-element.38), channel_id=1, source_target_pairs={{0,5},{1,6},{2,7},{3,0},{4,1},{5,2},{6,3},{7,4},{8,13},{9,14},{10,... | collective-permute-start | bytes 393224 | tf_op jit(solution)/shard_map/ppermute | solution.py:285
  35.0 0.0 copy-start.2
  35.0 4.8 %conv_outer.3 = (bf16[128,512]{1,0:T(8,128)(2,1)S(1)}, bf16[128,512]{1,0:T(8,128)(2,1)S(1)}, bf16[128,512]{1,0:T(8,128)(2,1)S(1)}, bf16[128,512]{1,0:T(8,128)(2,...) custom-call(s32[4,8]{1,0:T(4,128)S(1)} %constant_dynamic-slice_fusio, ...), custom_call_target="tpu_custom_call" | custom-call | flops 3422552064 | bytes 9437184 | tf_op jit(solution)/shard_map/conv_outer/pallas_call | solution.py:140
  39.8 0.0 collective-permute-done.10.refs_1_
  39.8 1.9 %collective-permute-start.15 = (bf16[128,512]{1,0:T(8,128)(2,1)S(1)}, bf16[128,512]{1,0:T(8,128)(2,1)S(1)}, u32[]{:S(2)}, u32[]{:S(2)}) collective-permute-start(bf16[128,512]{1,0:T(8,128)(2,1)S(1)} %get-tuple-element.39), channel_id=1, source_target_pairs={{0,6},{1,7},{2,0},{3,1},{4,2},{5,3},{6,4},{7,5},{8,14},{9,15},{10,... | collective-permute-start | bytes 393224 | tf_op jit(solution)/shard_map/ppermute | solution.py:285
  41.7 0.0 collective-permute-done.11.refs_2_
  41.7 0.7 collective-permute-start.16
  42.4 0.0 collective-permute-done.12.refs_3_
  42.4 1.0 collective-permute-start.3
  43.4 0.0 collective-permute-done.13.refs_4_
  43.4 0.0 collective-permute-start.4
  43.4 0.5 collective-permute-done.14.refs_5_
  44.0 1.1 collective-permute-start.5
  45.1 0.0 collective-permute-done.15.refs_6_
  45.1 2.1 %collective-permute-start.6 = (bf16[128,512]{1,0:T(8,128)(2,1)S(1)}, bf16[128,512]{1,0:T(8,128)(2,1)S(1)}, u32[]{:S(2)}, u32[]{:S(2)}) collective-permute-start(bf16[128,512]{1,0:T(8,128)(2,1)S(1)} %get-tuple-element.29), channel_id=1, source_target_pairs={{0,4},{1,5},{2,6},{3,7},{4,0},{5,1},{6,2},{7,3},{8,12},{9,13},{10,... | collective-permute-start | bytes 393224 | tf_op jit(solution)/shard_map/ppermute | solution.py:285
  47.2 0.0 collective-permute-done.16.refs_7_
  47.2 2.0 %collective-permute-start.7 = (bf16[128,512]{1,0:T(8,128)(2,1)S(1)}, bf16[128,512]{1,0:T(8,128)(2,1)S(1)}, u32[]{:S(2)}, u32[]{:S(2)}) collective-permute-start(bf16[128,512]{1,0:T(8,128)(2,1)S(1)} %get-tuple-element.30), channel_id=1, source_target_pairs={{0,5},{1,6},{2,7},{3,0},{4,1},{5,2},{6,3},{7,4},{8,13},{9,14},{10,... | collective-permute-start | bytes 393224 | tf_op jit(solution)/shard_map/ppermute | solution.py:285
  49.2 0.0 collective-permute-done.3.refs_1_
  49.2 0.3 collective-permute-start.8
  49.5 2.1 %collective-permute-done.4.refs_2_ = bf16[128,512]{1,0:T(8,128)(2,1)S(1)} collective-permute-done((bf16[128,512]{1,0:T(8,128)(2,1)S(1)}, bf16[128,512]{1,0:T(8,128)(2,1)S(1)}, u32[]{:S(2)}, u32[]{:S(2)}) %collective-permute-start.4) | collective-permute-done | bytes 131104 | tf_op jit(solution)/shard_map/ppermute | solution.py:285
  51.6 0.0 collective-permute-start.9
  51.6 0.0 copy-done.2
  51.6 7.2 %frame_attention.2.refs_9_ = bf16[8,128,512]{2,1,0:T(8,128)(2,1)S(1)} custom-call(s32[8]{0:T(128)S(1)} %compare_select_fusion.place_ref, bf16[128,512]{1,0:T(8,128)(2,1)S(1)} %get-tuple-element.33.refs_0_, bf16[128,512]{1,0:T(8,128)(2,1)S(1)} %collective-permute-done.10.refs_1_, bf16[128,512]{1,0:T(8,128)(2,1)S(1)} %collective-permute-done.11.refs_2_, ...), custom_call_target="tpu_custom_call" | custom-call | flops 4294967296 | bytes 4194304 | tf_op jit(solution)/shard_map/frame_attention/pallas_call | solution.py:206
  58.9 0.0 collective-permute-done.5.refs_3_
  58.9 0.0 collective-permute-done.6.refs_4_
  58.9 0.0 collective-permute-done.7.refs_5_
  58.9 0.0 collective-permute-done.8.refs_6_
  58.9 0.0 collective-permute-done.9.refs_7_
  59.0 8.6 %frame_attention.3 = bf16[8,256,512]{2,1,0:T(8,128)(2,1)} custom-call(s32[8]{0:T(128)S(1)} %compare_select_fusion.place_ref, bf16[128,512]{1,0:T(8,128)(2,1)S(1)} %get-tuple-element.25.refs_9_.refs_0_, bf16[128,512]{1,0:T(8,128)(2,1)S(1)} %collective-permute-done.3.refs_1_, bf16[128,512]{1,0:T(8,128)(2,1)S(1)} %collective-permute-done.4.refs_2_, ...), custom_call_target="tpu_custom_call" | custom-call | flops 4294967296 | bytes 4194304 | tf_op jit(solution)/shard_map/frame_attention/pallas_call | solution.py:206
  67.5 14.2 %all-to-all-start = ((bf16[128,16,512]{2,1,0:T(8,128)(2,1)}), bf16[128,16,512]{2,1,0:T(8,128)(2,1)S(1)}, u32[]{:S(2)}, u32[]{:S(2)}) async-start(bf16[128,16,512]{2,1,0:T(8,128)(2,1)} %bitcast.11), calls=%async_computation | async-start | bytes 4194304 | tf_op jit(solution)/shard_map/all_to_all | solution.py:316
  81.7 0.1 fusion.1.bias_ref
  81.8 29.5 %all-to-all-done = bf16[128,16,512]{2,1,0:T(8,128)(2,1)S(1)} async-done(((bf16[128,16,512]{2,1,0:T(8,128)(2,1)}), bf16[128,16,512]{2,1,0:T(8,128)(2,1)S(1)}, u32[]{:S(2)}, u32[]{:S(2)}) %all-to-all-start) | async-done | bytes 2097184 | tf_op jit(solution)/shard_map/all_to_all | solution.py:316
  111.4 0.0 copy-start.3
  111.4 1.6 %copy-done.3 = bf16[4,512,512]{2,1,0:T(8,128)(2,1)S(1)} copy-done((bf16[4,512,512]{2,1,0:T(8,128)(2,1)S(1)}, bf16[4,512,512]{2,1,0:T(8,128)(2,1)}, u32[]{:S(2)}) %copy-start.3) | copy-done | bytes 2097176
  112.9 12.2 %time_attention.1 = bf16[256,4,2,512]{3,2,1,0:T(2,128)(2,1)} custom-call(bf16[8,256,512]{2,1,0:T(8,128)(2,1)S(1)} %bitcast.27, f32[256,256]{1,0:T(8,128)S(1)} %fusion.1.bias_ref, bf16[4,512,512]{2,1,0:T(8,128)(2,1)S(1)} %copy-done.3), custom_call_target="tpu_custom_call" | custom-call | flops 5368709120 | bytes 6291456 | tf_op jit(solution)/shard_map/time_attention/pallas_call | solution.py:263
  (2 shorter events, 0.0 us)
Async XLA Ops:
  0.0 9.5 %copy-start = (bf16[16,4,32,512]{3,2,1,0:T(8,128)(2,1)S(1)}, bf16[16,4,32,512]{3,2,1,0:T(8,128)(2,1)}, u32[]{:S(2)}) copy-start(bf16[16,4,32,512]{3,2,1,0:T(8,128)(2,1)} %param.6) | copy-start | bytes 6291460
  0.0 9.0 %copy-start.5 = (s32[256]{0:T(256)S(1)}, s32[256]{0:T(256)}, u32[]{:S(2)}) copy-start(s32[256]{0:T(256)} %param.7) | copy-start | bytes 3076
  2.5 14.8 %collective-permute-start = (bf16[16,32,512]{2,1,0:T(8,128)(2,1)}, bf16[16,32,512]{2,1,0:T(8,128)(2,1)S(1)}, u32[]{:S(2)}, u32[]{:S(2)}) collective-permute-start(bf16[16,32,512]{2,1,0:T(8,128)(2,1)} %get-tuple-element.44), channel_id=1, source_target_pairs={{0,1},{1,2},{2,3},{3,4},{4,5},{5,6},{6,7},{8,9},{9,10},{10,11},{11... | collective-permute-start | bytes 1572872 | tf_op jit(solution)/shard_map/ppermute | solution.py:289
  7.1 10.7 %collective-permute-start.1 = (bf16[16,32,512]{2,1,0:T(8,128)(2,1)}, bf16[16,32,512]{2,1,0:T(8,128)(2,1)S(1)}, u32[]{:S(2)}, u32[]{:S(2)}) collective-permute-start(bf16[16,32,512]{2,1,0:T(8,128)(2,1)} %get-tuple-element.43), channel_id=1, source_target_pairs={{1,0},{2,1},{3,2},{4,3},{5,4},{6,5},{7,6},{9,8},{10,9},{11,10},{12... | collective-permute-start | bytes 1572872 | tf_op jit(solution)/shard_map/ppermute | solution.py:290
  9.5 2.3 %copy-start.1 = (bf16[9,512,512]{2,1,0:T(8,128)(2,1)S(1)}, bf16[9,512,512]{2,1,0:T(8,128)(2,1)}, u32[]{:S(2)}) copy-start(bf16[9,512,512]{2,1,0:T(8,128)(2,1)} %refs_2_.1) | copy-start | bytes 14155780
  11.9 5.9 %copy-start.4 = (bf16[3,512,512]{2,1,0:T(8,128)(2,1)S(1)}, bf16[3,512,512]{2,1,0:T(8,128)(2,1)}, u32[]{:S(2)}) copy-start(bf16[3,512,512]{2,1,0:T(8,128)(2,1)} %refs_3_.1) | copy-start | bytes 4718596
  23.9 8.7 %collective-permute-start.2 = (bf16[2,128,512]{2,1,0:T(8,128)(2,1)S(1)}, bf16[2,128,512]{2,1,0:T(8,128)(2,1)S(1)}, u32[]{:S(2)}, u32[]{:S(2)}) collective-permute-start(bf16[2,128,512]{2,1,0:T(8,128)(2,1)S(1)} %get-tuple-element.24), channel_id=1, source_target_pairs={{0,8},{8,16},{16,24},{24,32},{32,40},{40,48},{48,56},{56,64},{64,7... | collective-permute-start | bytes 786440 | tf_op jit(solution)/shard_map/ppermute | solution.py:307
  27.6 12.2 %collective-permute-start.10 = (bf16[128,512]{1,0:T(8,128)(2,1)S(1)}, bf16[128,512]{1,0:T(8,128)(2,1)S(1)}, u32[]{:S(2)}, u32[]{:S(2)}) collective-permute-start(bf16[128,512]{1,0:T(8,128)(2,1)S(1)} %get-tuple-element.34), channel_id=1, source_target_pairs={{0,1},{1,2},{2,3},{3,4},{4,5},{5,6},{6,7},{7,0},{8,9},{9,10},{10,1... | collective-permute-start | bytes 393224 | tf_op jit(solution)/shard_map/ppermute | solution.py:285
  29.2 12.5 %collective-permute-start.11 = (bf16[128,512]{1,0:T(8,128)(2,1)S(1)}, bf16[128,512]{1,0:T(8,128)(2,1)S(1)}, u32[]{:S(2)}, u32[]{:S(2)}) collective-permute-start(bf16[128,512]{1,0:T(8,128)(2,1)S(1)} %get-tuple-element.35), channel_id=1, source_target_pairs={{0,2},{1,3},{2,4},{3,5},{4,6},{5,7},{6,0},{7,1},{8,10},{9,11},{10,... | collective-permute-start | bytes 393224 | tf_op jit(solution)/shard_map/ppermute | solution.py:285
  30.5 11.9 %collective-permute-start.12 = (bf16[128,512]{1,0:T(8,128)(2,1)S(1)}, bf16[128,512]{1,0:T(8,128)(2,1)S(1)}, u32[]{:S(2)}, u32[]{:S(2)}) collective-permute-start(bf16[128,512]{1,0:T(8,128)(2,1)S(1)} %get-tuple-element.36), channel_id=1, source_target_pairs={{0,3},{1,4},{2,5},{3,6},{4,7},{5,0},{6,1},{7,2},{8,11},{9,12},{10,... | collective-permute-start | bytes 393224 | tf_op jit(solution)/shard_map/ppermute | solution.py:285
  32.1 11.3 %collective-permute-start.13 = (bf16[128,512]{1,0:T(8,128)(2,1)S(1)}, bf16[128,512]{1,0:T(8,128)(2,1)S(1)}, u32[]{:S(2)}, u32[]{:S(2)}) collective-permute-start(bf16[128,512]{1,0:T(8,128)(2,1)S(1)} %get-tuple-element.37), channel_id=1, source_target_pairs={{0,4},{1,5},{2,6},{3,7},{4,0},{5,1},{6,2},{7,3},{8,12},{9,13},{10,... | collective-permute-start | bytes 393224 | tf_op jit(solution)/shard_map/ppermute | solution.py:285
  32.6 11.4 %collective-permute-start.14 = (bf16[128,512]{1,0:T(8,128)(2,1)S(1)}, bf16[128,512]{1,0:T(8,128)(2,1)S(1)}, u32[]{:S(2)}, u32[]{:S(2)}) collective-permute-start(bf16[128,512]{1,0:T(8,128)(2,1)S(1)} %get-tuple-element.38), channel_id=1, source_target_pairs={{0,5},{1,6},{2,7},{3,0},{4,1},{5,2},{6,3},{7,4},{8,13},{9,14},{10,... | collective-permute-start | bytes 393224 | tf_op jit(solution)/shard_map/ppermute | solution.py:285
  35.0 16.7 %copy-start.2 = (bf16[4,512,512]{2,1,0:T(8,128)(2,1)S(1)}, bf16[4,512,512]{2,1,0:T(8,128)(2,1)}, u32[]{:S(2)}) copy-start(bf16[4,512,512]{2,1,0:T(8,128)(2,1)} %refs_8_.3) | copy-start | bytes 6291460
  39.8 5.3 %collective-permute-start.15 = (bf16[128,512]{1,0:T(8,128)(2,1)S(1)}, bf16[128,512]{1,0:T(8,128)(2,1)S(1)}, u32[]{:S(2)}, u32[]{:S(2)}) collective-permute-start(bf16[128,512]{1,0:T(8,128)(2,1)S(1)} %get-tuple-element.39), channel_id=1, source_target_pairs={{0,6},{1,7},{2,0},{3,1},{4,2},{5,3},{6,4},{7,5},{8,14},{9,15},{10,... | collective-permute-start | bytes 393224 | tf_op jit(solution)/shard_map/ppermute | solution.py:285
  41.7 5.5 %collective-permute-start.16 = (bf16[128,512]{1,0:T(8,128)(2,1)S(1)}, bf16[128,512]{1,0:T(8,128)(2,1)S(1)}, u32[]{:S(2)}, u32[]{:S(2)}) collective-permute-start(bf16[128,512]{1,0:T(8,128)(2,1)S(1)} %get-tuple-element.40), channel_id=1, source_target_pairs={{0,7},{1,0},{2,1},{3,2},{4,3},{5,4},{6,5},{7,6},{8,15},{9,8},{10,9... | collective-permute-start | bytes 393224 | tf_op jit(solution)/shard_map/ppermute | solution.py:285
  42.4 6.8 %collective-permute-start.3 = (bf16[128,512]{1,0:T(8,128)(2,1)S(1)}, bf16[128,512]{1,0:T(8,128)(2,1)S(1)}, u32[]{:S(2)}, u32[]{:S(2)}) collective-permute-start(bf16[128,512]{1,0:T(8,128)(2,1)S(1)} %get-tuple-element.26), channel_id=1, source_target_pairs={{0,1},{1,2},{2,3},{3,4},{4,5},{5,6},{6,7},{7,0},{8,9},{9,10},{10,1... | collective-permute-start | bytes 393224 | tf_op jit(solution)/shard_map/ppermute | solution.py:285
  43.4 8.2 %collective-permute-start.4 = (bf16[128,512]{1,0:T(8,128)(2,1)S(1)}, bf16[128,512]{1,0:T(8,128)(2,1)S(1)}, u32[]{:S(2)}, u32[]{:S(2)}) collective-permute-start(bf16[128,512]{1,0:T(8,128)(2,1)S(1)} %get-tuple-element.27), channel_id=1, source_target_pairs={{0,2},{1,3},{2,4},{3,5},{4,6},{5,7},{6,0},{7,1},{8,10},{9,11},{10,... | collective-permute-start | bytes 393224 | tf_op jit(solution)/shard_map/ppermute | solution.py:285
  44.0 14.9 %collective-permute-start.5 = (bf16[128,512]{1,0:T(8,128)(2,1)S(1)}, bf16[128,512]{1,0:T(8,128)(2,1)S(1)}, u32[]{:S(2)}, u32[]{:S(2)}) collective-permute-start(bf16[128,512]{1,0:T(8,128)(2,1)S(1)} %get-tuple-element.28), channel_id=1, source_target_pairs={{0,3},{1,4},{2,5},{3,6},{4,7},{5,0},{6,1},{7,2},{8,11},{9,12},{10,... | collective-permute-start | bytes 393224 | tf_op jit(solution)/shard_map/ppermute | solution.py:285
  45.1 13.8 %collective-permute-start.6 = (bf16[128,512]{1,0:T(8,128)(2,1)S(1)}, bf16[128,512]{1,0:T(8,128)(2,1)S(1)}, u32[]{:S(2)}, u32[]{:S(2)}) collective-permute-start(bf16[128,512]{1,0:T(8,128)(2,1)S(1)} %get-tuple-element.29), channel_id=1, source_target_pairs={{0,4},{1,5},{2,6},{3,7},{4,0},{5,1},{6,2},{7,3},{8,12},{9,13},{10,... | collective-permute-start | bytes 393224 | tf_op jit(solution)/shard_map/ppermute | solution.py:285
  47.2 11.7 %collective-permute-start.7 = (bf16[128,512]{1,0:T(8,128)(2,1)S(1)}, bf16[128,512]{1,0:T(8,128)(2,1)S(1)}, u32[]{:S(2)}, u32[]{:S(2)}) collective-permute-start(bf16[128,512]{1,0:T(8,128)(2,1)S(1)} %get-tuple-element.30), channel_id=1, source_target_pairs={{0,5},{1,6},{2,7},{3,0},{4,1},{5,2},{6,3},{7,4},{8,13},{9,14},{10,... | collective-permute-start | bytes 393224 | tf_op jit(solution)/shard_map/ppermute | solution.py:285
  49.2 9.7 %collective-permute-start.8 = (bf16[128,512]{1,0:T(8,128)(2,1)S(1)}, bf16[128,512]{1,0:T(8,128)(2,1)S(1)}, u32[]{:S(2)}, u32[]{:S(2)}) collective-permute-start(bf16[128,512]{1,0:T(8,128)(2,1)S(1)} %get-tuple-element.31), channel_id=1, source_target_pairs={{0,6},{1,7},{2,0},{3,1},{4,2},{5,3},{6,4},{7,5},{8,14},{9,15},{10,... | collective-permute-start | bytes 393224 | tf_op jit(solution)/shard_map/ppermute | solution.py:285
  51.6 7.3 %collective-permute-start.9 = (bf16[128,512]{1,0:T(8,128)(2,1)S(1)}, bf16[128,512]{1,0:T(8,128)(2,1)S(1)}, u32[]{:S(2)}, u32[]{:S(2)}) collective-permute-start(bf16[128,512]{1,0:T(8,128)(2,1)S(1)} %get-tuple-element.32), channel_id=1, source_target_pairs={{0,7},{1,0},{2,1},{3,2},{4,3},{5,4},{6,5},{7,6},{8,15},{9,8},{10,9... | collective-permute-start | bytes 393224 | tf_op jit(solution)/shard_map/ppermute | solution.py:285
  67.5 43.8 %all-to-all-start = ((bf16[128,16,512]{2,1,0:T(8,128)(2,1)}), bf16[128,16,512]{2,1,0:T(8,128)(2,1)S(1)}, u32[]{:S(2)}, u32[]{:S(2)}) async-start(bf16[128,16,512]{2,1,0:T(8,128)(2,1)} %bitcast.11), calls=%async_computation | async-start | bytes 4194304 | tf_op jit(solution)/shard_map/all_to_all | solution.py:316
  111.4 1.6 %copy-start.3 = (bf16[4,512,512]{2,1,0:T(8,128)(2,1)S(1)}, bf16[4,512,512]{2,1,0:T(8,128)(2,1)}, u32[]{:S(2)}) copy-start(bf16[4,512,512]{2,1,0:T(8,128)(2,1)} %w_ref.3) | copy-start | bytes 6291460

commit v3 on v2

--- a/solution.py
+++ b/solution.py
@@ -5,7 +5,7 @@
 from jax import lax
 from jax.experimental import pallas as pl
 from jax.experimental.pallas import tpu as pltpu
-from jax.sharding import PartitionSpec as P
+from jax.sharding import Mesh, PartitionSpec as P
 
 GROUPS = 32
 EPS = 1e-06
@@ -122,7 +122,8 @@
         y = mm(jnp.concatenate(taps, axis=1), weights)
         for s in range(per):
             own = y[s * tokens : (s + 1) * tokens] + x_ref[idx_ref[3, s0 + s]].astype(F32)
-            outs[s0 + s][...] = mm(order, own.astype(BF)).astype(BF)
+            k = s0 + s
+            outs[k // 2][(k % 2) * tokens : (k % 2 + 1) * tokens] = mm(order, own.astype(BF)).astype(BF)
     if late:
         lead_ref[...] = hs[0:2]
         tail_ref[...] = hs[8:10]
@@ -133,7 +134,7 @@
     count = 10 if late else 6
     ins = [x, up, dn, inner, *given, w_space, w_time]
     vmem = pl.BlockSpec(memory_space=pltpu.VMEM)
-    out_shape = [jax.ShapeDtypeStruct((tokens, c), BF)] * 8
+    out_shape = [jax.ShapeDtypeStruct((2 * tokens, c), BF)] * 4
     if late:
         out_shape = out_shape + [jax.ShapeDtypeStruct((2, tokens, c), BF)] * 2
     rows = count * 64
@@ -168,49 +169,55 @@
 
 
 def frame_kernel(pair, place_ref, *refs):
-    xs, (w_ref, other_ref, out_ref, q_s, k_s, v_s) = refs[:8], refs[8:]
-    block, c = xs[0].shape
-    tokens = 8 * block
+    owns, (twins_ref, w_ref, other_ref, out_ref, x_s, q_s, k_s, v_s) = refs[:4], refs[4:]
+    block, c = twins_ref.shape[1:]
+    rows = 2 * block
+    tokens = 4 * rows
     per_group = c // GROUPS
     entries = tokens * per_group
 
     sums, squares = 0.0, 0.0
-    for ref in xs:
-        values = ref[...].astype(F32)
+    for s in range(4):
+        x = jnp.concatenate([owns[s][0:block], twins_ref[s]], axis=0)
+        x_s[s * rows : (s + 1) * rows] = x
+        values = x.astype(F32)
         sums = sums + jnp.sum(values, axis=0, keepdims=True)
         squares = squares + jnp.sum(values * values, axis=0, keepdims=True)
     both = group_sum(jnp.concatenate([sums, squares] * 4, axis=0), per_group) / entries
     average, square = both[0:1], both[1:2]
     inverse = lax.rsqrt(square - average * average + EPS)
-    for s in range(0, 8, 2):
-        values = jnp.concatenate([xs[s][...], xs[s + 1][...]], axis=0).astype(F32)
-        normed = ((values - average) * inverse).astype(BF)
+    for s in range(4):
+        span = slice(s * rows, (s + 1) * rows)
+        normed = ((x_s[span].astype(F32) - average) * inverse).astype(BF)
         for i, ref in enumerate((q_s, k_s, v_s)):
-            ref[s * block : (s + 2) * block] = mm(normed, w_ref[i]).astype(BF)
-    for s in range(0, 8, 2):
-        q = q_s[s * block : (s + 2) * block]
-        probs = softmax_rows(mm_nt(q, k_s[...]), c ** (-0.5) * LOG2E)
-        y = mm(mm(probs, v_s[...]).astype(BF), w_ref[3])
-        for k in range(2):
-            part = y[k * block : (k + 1) * block] + xs[s + k][...].astype(F32)
+            ref[span] = mm(normed, w_ref[i]).astype(BF)
+    spans = [slice(s * rows, (s + 1) * rows) for s in range(4)]
+    scores = [mm_nt(q_s[span], k_s[...]) for span in spans]
+    probs = [softmax_rows(s, c ** (-0.5) * LOG2E) for s in scores]
+    mixes = [mm(p, v_s[...]).astype(BF) for p in probs]
+    for s in range(4):
+        y = mm(mixes[s], w_ref[3]) + x_s[spans[s]].astype(F32)
+        for core in range(2):
+            part = y[core * block : (core + 1) * block]
+            place = place_ref[core, s]
             if pair:
-                other = other_ref[place_ref[s + k]].astype(F32).reshape(block // 8, 8, c)
+                other = other_ref[place].astype(F32).reshape(block // 8, 8, c)
                 part = jnp.concatenate([part.reshape(block // 8, 8, c), other], axis=1)
-            out_ref[place_ref[s + k]] = part.reshape(-1, c).astype(BF)
-
-
-def frame_attention(pair, place, xs, weights, other):
-    block, c = xs[0].shape
+            out_ref[place] = part.reshape(-1, c).astype(BF)
+
+
+def frame_attention(pair, place, owns, twins, weights, other):
+    block, c = twins.shape[1:]
     tokens = 8 * block
     vmem = pl.BlockSpec(memory_space=pltpu.VMEM)
     return pl.pallas_call(
         functools.partial(frame_kernel, pair),
         out_shape=jax.ShapeDtypeStruct((8, block * (2 if pair else 1), c), BF),
         in_specs=[pl.BlockSpec(memory_space=pltpu.SMEM)]
-        + [vmem] * 9
+        + [vmem] * 6
         + [vmem if pair else pl.BlockSpec(memory_space=pl.ANY)],
         out_specs=vmem,
-        scratch_shapes=[pltpu.VMEM((tokens, c), BF)] * 3,
+        scratch_shapes=[pltpu.VMEM((tokens, c), BF)] * 4,
         compiler_params=pltpu.CompilerParams(vmem_limit_bytes=VMEM_LIMIT),
         cost_estimate=pl.CostEstimate(
             flops=8 * tokens * c * c + 4 * tokens * tokens * c,
@@ -218,7 +225,7 @@
             transcendentals=tokens * tokens,
         ),
         name="frame_attention",
-    )(place, *xs, weights, other)
+    )(place, *owns, twins, weights, other)
 
 
 def by_cell(o):
@@ -240,21 +247,24 @@
 
 def time_kernel(x_ref, bias_ref, w_ref, out_ref, x_s, q_s, k_s, v_s):
     c = x_ref.shape[-1]
-    order = one_hot_rows(256, by_cell)
-    for u in range(8):
-        span = slice(32 * u, 32 * u + 32)
-        x = mm(order, x_ref[:, span, :].reshape(256, c)).astype(BF)
-        for ref, value in zip((x_s, q_s, k_s, v_s), [x, *project_time(x, w_ref)]):
+    spans = [slice(32 * u, 32 * u + 32) for u in range(8)]
+    order, back = one_hot_rows(256, by_cell), one_hot_rows(256, by_frame)
+    for span in spans:
+        x_s[:, span, :] = mm(order, x_ref[:, span, :].reshape(256, c)).astype(BF).reshape(8, 32, c)
+    for span in spans:
+        parts = project_time(x_s[:, span, :].reshape(256, c), w_ref)
+        for ref, value in zip((q_s, k_s, v_s), parts):
             ref[:, span, :] = value.reshape(8, 32, c)
-    for cell in range(8):
-        scores = mm_nt(q_s[cell], k_s[cell]) * (c ** (-0.5) * LOG2E) + bias_ref[...]
-        q_s[cell] = mm(softmax_rows(scores, 1.0), v_s[cell]).astype(BF)
-    back = one_hot_rows(256, by_frame)
-    for u in range(8):
-        span = slice(32 * u, 32 * u + 32)
+    scores = [mm_nt(q_s[i], k_s[i]) * (c ** (-0.5) * LOG2E) + bias_ref[...] for i in range(8)]
+    probs = [softmax_rows(s, 1.0) for s in scores]
+    for i in range(8):
+        q_s[i] = mm(probs[i], v_s[i]).astype(BF)
+    for span in spans:
         y = mm(q_s[:, span, :].reshape(256, c), w_ref[3])
         y = (y + x_s[:, span, :].reshape(256, c).astype(F32)).astype(BF)
-        out_ref[span] = mm(back, y).astype(BF).reshape(32, 4, 2, c)
+        k_s[:, span, :] = y.reshape(8, 32, c)
+    for span in spans:
+        out_ref[span] = mm(back, k_s[:, span, :].reshape(256, c)).astype(BF).reshape(32, 4, 2, c)
 
 
 def time_attention(x, bias, weights):
@@ -278,16 +288,16 @@
 
 def shards(video, video_ids, w_space, w_time, spatial_attn, time_attn):
     frames, rows, cols, c = video.shape
-    tm_count, rows_count = lax.axis_size("tm"), lax.axis_size("rows")
+    tm_count, y_count = lax.axis_size("tm"), lax.axis_size("y")
     half = frames // 2
     tokens = rows * cols
-    me = lax.axis_index("rows")
-    around = lambda a, by: lax.ppermute(
-        a, "rows", [(i, (i + by) % rows_count) for i in range(rows_count)]
-    )
-
-    up = lax.ppermute(video[:, rows - 1], "rows", [(i, i + 1) for i in range(rows_count - 1)])
-    dn = lax.ppermute(video[:, 0], "rows", [(i + 1, i) for i in range(rows_count - 1)])
+    y, core = lax.axis_index("y"), lax.axis_index("core")
+    row_axes = ("y", "core")
+    row_count = 2 * y_count
+    swapped = lambda a: lax.ppermute(a, "core", [(0, 1), (1, 0)])
+
+    up = lax.ppermute(video[:, rows - 1], row_axes, [(i, i + 1) for i in range(row_count - 1)])
+    dn = lax.ppermute(video[:, 0], row_axes, [(i + 1, i) for i in range(row_count - 1)])
     x = video.reshape(frames, tokens, c)
     inner = conv_inner(x, w_space)
 
@@ -296,26 +306,33 @@
     place = jnp.arange(frames, dtype=jnp.int32) % half
     one = jnp.where(ids[1:-1] == ids[2:], place + 1, place + 2)
     two = jnp.where(ids[:-2] == ids[2:], place, one)
+    steps = jnp.arange(y_count, dtype=jnp.int32)
+    ahead = 2 * lax.rem(y + steps, y_count)
+    goes = jnp.stack([ahead + core, ahead + 1 - core], axis=1).reshape(-1)
+    behind = 2 * lax.rem(y - steps + y_count, y_count)
+    place_of = jnp.stack([behind + core, behind + 1 - core])
 
     def slots(late):
         own = slice(half, frames) if late else slice(0, half)
         first = half if late else 0
         table = jnp.stack([place[own] + 2, one[own], two[own], place[own] + first])
-        return lax.dynamic_slice_in_dim(jnp.concatenate([table, table], axis=1), me, half, axis=1)
+        chosen = goes[:, None] == jnp.arange(half, dtype=jnp.int32)[None, :]
+        return jnp.sum(jnp.where(chosen[None], table[:, None, :], 0), axis=2)
+
+    def exchanged(blocks):
+        turn = lambda s: [(i, (i + s) % y_count) for i in range(y_count)]
+        owns = [blocks[0]] + [lax.ppermute(blocks[s], "y", turn(s)) for s in range(1, y_count)]
+        return owns, swapped(jnp.stack([a[tokens:] for a in owns]))
 
     *late, lead, tail = conv_outer(True, slots(True), x, up, dn, inner, [], w_space, w_time)
     tail = lax.ppermute(tail, "tm", [(t, t + 1) for t in range(tm_count - 1)])
     early = conv_outer(False, slots(False), x, up, dn, inner, [lead, tail], w_space, w_time)
 
-    sources = lax.rem(me - jnp.arange(rows_count, dtype=jnp.int32) + rows_count, rows_count)
-    def exchanged(conv):
-        return [conv[0]] + [around(conv[s], s) for s in range(1, rows_count)]
-
-    done = frame_attention(False, sources, exchanged(late), spatial_attn, early[0])
-    done = frame_attention(True, sources, exchanged(early), spatial_attn, done)
+    done = frame_attention(False, place_of, *exchanged(late), spatial_attn, early[0])
+    done = frame_attention(True, place_of, *exchanged(early), spatial_attn, done)
     arrived = lax.all_to_all(
-        done.reshape(rows_count * tm_count, -1, c), ("rows", "tm"), 0, 0, tiled=True
-    ).reshape(rows_count, -1, c)
+        done.reshape(row_count * tm_count, -1, c), ("y", "core", "tm"), 0, 0, tiled=True
+    ).reshape(row_count, -1, c)
 
     number = jnp.arange(frames * tm_count, dtype=jnp.int32)
     allowed = (number[None, :] <= number[:, None]) & (video_ids[None, :] == video_ids[:, None])
@@ -323,6 +340,8 @@
 
 
 def solution(mesh):
-    in_specs = (P("tm", "rows", None, None), P(), P(), P(), P(), P())
-    out_specs = P(None, "rows", "tm", None)
+    mesh = Mesh(mesh.devices.reshape(mesh.devices.shape[0], -1, 2), ("tm", "y", "core"))
+    rows = ("y", "core")
+    in_specs = (P("tm", rows, None, None), P(), P(), P(), P(), P())
+    out_specs = P(None, rows, "tm", None)
     return jax.shard_map(shards, mesh=mesh, in_specs=in_specs, out_specs=out_specs, check_vma=False)

time: 125 us -> 118 us (0.944)
  starting transfers between devices: 40.7 us -> 33.8 us
  Pallas kernels: 44.4 us -> 37.8 us
  waiting for transfers between devices: 32.8 us -> 37.9 us
    ppermute x16 -> x10, waiting for transfers between devices: 3.22 us -> 8.36 us  [the longest x6 8.19 us: exchanged(): lax.ppermute(blocks[s], 'y', turn(s))]
    all_to_all x1, starting transfers between devices: 14.2 us -> 9.4 us  [shards(): lax.all_to_all(done.reshape(row_count * tm_count, -1, c), ('y', 'core', '...]
    pallas_call x1, Pallas kernels: 12.2 us -> 8.64 us  [time_attention(): pl.pallas_call(time_kernel, out_shape=jax.ShapeDtypeStruct((256, 4, 2, c)...]
    pallas_call x2, Pallas kernels: 15.8 us -> 12.9 us  [frame_attention(): pl.pallas_call(functools.partial(frame_kernel, pair), out_shape=jax.Shape...]
    ppermute x16 -> x10, starting transfers between devices: 23 us -> 20.8 us  [the longest x6 11.5 us: exchanged(): lax.ppermute(blocks[s], 'y', turn(s))]
    unnamed x12 -> x14, local copies, waits for them, and re-layouts: 3.95 us -> 3.94 us
  transfers between devices with their start and end apart: 18 -> 12, of which waited for: 4 -> 4; matrix products, arithmetic and copies ran while one was open for 1% -> 1% of each run, Pallas kernels for 14% -> 14%
where the time goes in v3:
time: 118 us; the launch traced here: 117 us
  waiting for transfers between devices  37.9 us (32%)
  Pallas kernels  37.8 us (32%)
  starting transfers between devices  33.8 us (29%)
  local copies, waits for them, and re-layouts  6.78 us (6%)
    all_to_all x1, waiting for transfers between devices, shards(): lax.all_to_all(done.reshape(row_count * tm_count, -1, c), ('y', 'core', '...  29.5 us
    pallas_call x2, Pallas kernels, frame_attention(): pl.pallas_call(functools.partial(frame_kernel, pair), out_shape=jax.Shape...  12.9 us
    ppermute x6, starting transfers between devices, exchanged(): lax.ppermute(blocks[s], 'y', turn(s))  11.5 us
    pallas_call x2, Pallas kernels, conv_outer(): pl.pallas_call(functools.partial(outer_kernel, late), out_shape=out_shape...  11 us
    all_to_all x1, starting transfers between devices, shards(): lax.all_to_all(done.reshape(row_count * tm_count, -1, c), ('y', 'core', '...  9.4 us
    pallas_call x1, Pallas kernels, time_attention(): pl.pallas_call(time_kernel, out_shape=jax.ShapeDtypeStruct((256, 4, 2, c)...  8.64 us
    ppermute x6, waiting for transfers between devices, exchanged(): lax.ppermute(blocks[s], 'y', turn(s))  8.19 us
    pallas_call x1, Pallas kernels, conv_inner(): pl.pallas_call(inner_kernel, out_shape=jax.ShapeDtypeStruct((frames, toke...  5.37 us
  transfers between devices with their start and end apart: 12, of which 4 were waited for; matrix products, arithmetic and copies ran while one was open for 1% of the time, Pallas kernels for 14%

profile of v3, /device:TPU:1, one launch (start us, length us, event | category | flops | bytes accessed | tf_op | source)
XLA Modules:
  0.0 117.4 jit_solution(7128277952399521092)
XLA Ops:
  0.0 0.0 copy-start
  0.0 0.0 copy-start.6
  0.0 2.4 %slice_bitcast_fusion = (bf16[16,32,512]{2,1,0:T(8,128)(2,1)}, bf16[16,32,512]{2,1,0:T(8,128)(2,1)}) fusion(bf16[16,4,32,512]{3,2,1,0:T(8,128)(2,1)} %param.6), kind=kLoop, calls=%fused_computation.2 | loop fusion | bytes 2097152 | tf_op jit(solution)/shard_map/squeeze | solution.py:300
  2.5 4.6 %collective-permute-start = (bf16[16,32,512]{2,1,0:T(8,128)(2,1)}, bf16[16,32,512]{2,1,0:T(8,128)(2,1)S(1)}, u32[]{:S(2)}, u32[]{:S(2)}) collective-permute-start(bf16[16,32,512]{2,1,0:T(8,128)(2,1)} %get-tuple-element.30), channel_id=1, source_target_pairs={{0,1},{1,2},{2,3},{3,4},{4,5},{5,6},{6,7},{8,9},{9,10},{10,11},{11... | collective-permute-start | bytes 1572872 | tf_op jit(solution)/shard_map/ppermute | solution.py:299
  7.0 1.9 %collective-permute-start.1 = (bf16[16,32,512]{2,1,0:T(8,128)(2,1)}, bf16[16,32,512]{2,1,0:T(8,128)(2,1)S(1)}, u32[]{:S(2)}, u32[]{:S(2)}) collective-permute-start(bf16[16,32,512]{2,1,0:T(8,128)(2,1)} %get-tuple-element.29), channel_id=1, source_target_pairs={{1,0},{2,1},{3,2},{4,3},{5,4},{6,5},{7,6},{9,8},{10,9},{11,10},{12... | collective-permute-start | bytes 1572872 | tf_op jit(solution)/shard_map/ppermute | solution.py:300
  9.0 0.1 add_bitcast_fusion.2
  9.1 0.0 copy-done.6
  9.1 0.1 pad_dynamic-slice_fusion
  9.1 0.1 compare_select_fusion.2
  9.2 0.1 slice_bitcast_fusion.12
  9.3 0.1 slice_bitcast_fusion.13
  9.4 0.1 pad_add_fusion
  9.5 0.1 eq.24
  9.5 0.1 iota_compare_fusion.1
  9.6 0.2 select_reduce_fusion
  9.9 0.0 copy-done
  9.9 0.0 copy-start.1
  9.9 2.3 %copy-done.1 = bf16[9,512,512]{2,1,0:T(8,128)(2,1)S(1)} copy-done((bf16[9,512,512]{2,1,0:T(8,128)(2,1)S(1)}, bf16[9,512,512]{2,1,0:T(8,128)(2,1)}, u32[]{:S(2)}) %copy-start.1) | copy-done | bytes 4718616
  12.2 0.0 copy-start.5
  12.2 5.4 %conv_inner.1.inner_ref = bf16[16,64,512]{2,1,0:T(8,128)(2,1)S(1)} custom-call(bf16[16,128,512]{2,1,0:T(8,128)(2,1)S(1)} %bitcast.44, bf16[9,512,512]{2,1,0:T(8,128)(2,1)S(1)} %copy-done.1), custom_call_target="tpu_custom_call" | custom-call | flops 4831838208 | bytes 8388608 | tf_op jit(solution)/shard_map/conv_inner/pallas_call | solution.py:74
  17.6 0.0 collective-permute-done.up_ref
  17.6 0.2 collective-permute-done.1.dn_ref
  17.8 0.0 copy-done.5
  17.8 0.0 copy-start.2
  17.8 6.1 %conv_outer.2 = (bf16[256,512]{1,0:T(8,128)(2,1)S(1)}, bf16[256,512]{1,0:T(8,128)(2,1)S(1)}, bf16[256,512]{1,0:T(8,128)(2,1)S(1)}, bf16[256,512]{1,0:T(8,128)(2,...) custom-call(s32[4,8]{1,0:T(4,128)S(1)} %get-tuple-element.25.idx_ref, ...), custom_call_target="tpu_custom_call" | custom-call | flops 4630511616 | bytes 9437184 | tf_op jit(solution)/shard_map/conv_outer/pallas_call | solution.py:141
  23.9 3.6 %collective-permute-start.2 = (bf16[2,128,512]{2,1,0:T(8,128)(2,1)S(1)}, bf16[2,128,512]{2,1,0:T(8,128)(2,1)S(1)}, u32[]{:S(2)}, u32[]{:S(2)}) collective-permute-start(bf16[2,128,512]{2,1,0:T(8,128)(2,1)S(1)} %get-tuple-element.16), channel_id=1, source_target_pairs={{0,8},{8,16},{16,24},{24,32},{32,40},{40,48},{48,56},{56,64},{64,7... | collective-permute-start | bytes 786440 | tf_op jit(solution)/shard_map/ppermute | solution.py:328
  27.5 1.4 %collective-permute-start.7 = (bf16[256,512]{1,0:T(8,128)(2,1)S(1)}, bf16[256,512]{1,0:T(8,128)(2,1)S(1)}, u32[]{:S(2)}, u32[]{:S(2)}) collective-permute-start(bf16[256,512]{1,0:T(8,128)(2,1)S(1)} %get-tuple-element.22), channel_id=1, source_target_pairs={{0,2},{2,4},{4,6},{6,0},{1,3},{3,5},{5,7},{7,1},{8,10},{10,12},{12... | collective-permute-start | bytes 786440 | tf_op jit(solution)/shard_map/ppermute | solution.py:324
  28.8 1.4 %collective-permute-start.8 = (bf16[256,512]{1,0:T(8,128)(2,1)S(1)}, bf16[256,512]{1,0:T(8,128)(2,1)S(1)}, u32[]{:S(2)}, u32[]{:S(2)}) collective-permute-start(bf16[256,512]{1,0:T(8,128)(2,1)S(1)} %get-tuple-element.23), channel_id=1, source_target_pairs={{0,4},{2,6},{4,0},{6,2},{1,5},{3,7},{5,1},{7,3},{8,12},{10,14},{12... | collective-permute-start | bytes 786440 | tf_op jit(solution)/shard_map/ppermute | solution.py:324
  30.3 2.0 %collective-permute-start.9 = (bf16[256,512]{1,0:T(8,128)(2,1)S(1)}, bf16[256,512]{1,0:T(8,128)(2,1)S(1)}, u32[]{:S(2)}, u32[]{:S(2)}) collective-permute-start(bf16[256,512]{1,0:T(8,128)(2,1)S(1)} %get-tuple-element.24), channel_id=1, source_target_pairs={{0,6},{2,0},{4,2},{6,4},{1,7},{3,1},{5,3},{7,5},{8,14},{10,8},{12,... | collective-permute-start | bytes 786440 | tf_op jit(solution)/shard_map/ppermute | solution.py:324
  32.2 0.0 collective-permute-done.2.refs_1_
  32.3 0.0 copy-done.2
  32.3 4.8 %conv_outer.3 = (bf16[256,512]{1,0:T(8,128)(2,1)S(1)}, bf16[256,512]{1,0:T(8,128)(2,1)S(1)}, bf16[256,512]{1,0:T(8,128)(2,1)S(1)}, bf16[256,512]{1,0:T(8,128)(2,1)S(1)}) custom-call(s32[4,8]{1,0:T(4,128)S(1)} %get-tuple-element.26.idx_ref, bf16[16,128,512]{2,1,0:T(8,128)(2,1)S(1)} %bitcast.46, bf16[16,32,512]{2,1,0:T(8,128)(2,1)S(1)} %collective-permute-done.up_ref, ...), custom_call_target="tpu_custom_call" | custom-call | flops 3422552064 | bytes 9437184 | tf_op jit(solution)/shard_map/conv_outer/pallas_call | solution.py:141
  37.1 0.0 copy-start.3
  37.1 1.8 %collective-permute-start.3 = (bf16[256,512]{1,0:T(8,128)(2,1)S(1)}, bf16[256,512]{1,0:T(8,128)(2,1)S(1)}, u32[]{:S(2)}, u32[]{:S(2)}) collective-permute-start(bf16[256,512]{1,0:T(8,128)(2,1)S(1)} %get-tuple-element.18), channel_id=1, source_target_pairs={{0,2},{2,4},{4,6},{6,0},{1,3},{3,5},{5,7},{7,1},{8,10},{10,12},{12... | collective-permute-start | bytes 786440 | tf_op jit(solution)/shard_map/ppermute | solution.py:324
  38.9 1.1 collective-permute-start.4
  40.0 2.9 %collective-permute-done.9.refs_3_ = bf16[256,512]{1,0:T(8,128)(2,1)S(1)} collective-permute-done((bf16[256,512]{1,0:T(8,128)(2,1)S(1)}, bf16[256,512]{1,0:T(8,128)(2,1)S(1)}, u32[]{:S(2)}, u32[]{:S(2)}) %collective-permute-start.9) | collective-permute-done | bytes 262176 | tf_op jit(solution)/shard_map/ppermute | solution.py:324
  42.9 3.9 %collective-permute-start.5 = (bf16[256,512]{1,0:T(8,128)(2,1)S(1)}, bf16[256,512]{1,0:T(8,128)(2,1)S(1)}, u32[]{:S(2)}, u32[]{:S(2)}) collective-permute-start(bf16[256,512]{1,0:T(8,128)(2,1)S(1)} %get-tuple-element.20), channel_id=1, source_target_pairs={{0,6},{2,0},{4,2},{6,4},{1,7},{3,1},{5,3},{7,5},{8,14},{10,8},{12,... | collective-permute-start | bytes 786440 | tf_op jit(solution)/shard_map/ppermute | solution.py:324
  46.8 0.0 collective-permute-done.8.refs_2_
  46.8 0.0 collective-permute-done.7.refs_1_
  46.9 0.1 pad_maximum_fusion.1
  46.9 1.1 collective-permute-start.10
  48.1 5.3 %collective-permute-done.5.refs_3_ = bf16[256,512]{1,0:T(8,128)(2,1)S(1)} collective-permute-done((bf16[256,512]{1,0:T(8,128)(2,1)S(1)}, bf16[256,512]{1,0:T(8,128)(2,1)S(1)}, u32[]{:S(2)}, u32[]{:S(2)}) %collective-permute-start.5) | collective-permute-done | bytes 262176 | tf_op jit(solution)/shard_map/ppermute | solution.py:324
  53.4 0.0 collective-permute-done.4.refs_2_
  53.4 0.0 collective-permute-done.3.refs_1_
  53.4 0.1 pad_maximum_fusion
  53.5 1.7 %collective-permute-start.6 = (bf16[4,128,512]{2,1,0:T(8,128)(2,1)S(1)}, bf16[4,128,512]{2,1,0:T(8,128)(2,1)S(1)}, u32[]{:S(2)}, u32[]{:S(2)}) collective-permute-start(bf16[4,128,512]{2,1,0:T(8,128)(2,1)S(1)} %pad_maximum_fusion), channel_id=1, source_target_pairs={{0,1},{1,0},{2,3},{3,2},{4,5},{5,4},{6,7},{7,6},{8,9},{9,8},{10,11... | collective-permute-start | bytes 1572872 | tf_op jit(solution)/shard_map/ppermute | solution.py:297
  55.2 0.0 collective-permute-done.10.refs_4_
  55.2 0.0 copy-done.3
  55.2 5.8 %frame_attention.2.refs_6_ = bf16[8,128,512]{2,1,0:T(8,128)(2,1)S(1)} custom-call(s32[2,4]{1,0:T(2,128)S(1)} %pad_add_fusion.3.place_ref, bf16[256,512]{1,0:T(8,128)(2,1)S(1)} %get-tuple-element.21.refs_0_, bf16[256,512]{1,0:T(8,128)(2,1)S(1)} %collective-permute-done.7.refs_1_, bf16[256,512]{1,0:T(8,128)(2,1)S(1)} %collective-permute-done.8.refs_2_, ...), custom_call_target="tpu_custom_call" | custom-call | flops 4294967296 | bytes 4194304 | tf_op jit(solution)/shard_map/frame_attention/pallas_call | solution.py:213
  61.0 0.0 collective-permute-done.6.refs_4_
  61.0 7.1 %frame_attention.3 = bf16[8,256,512]{2,1,0:T(8,128)(2,1)} custom-call(s32[2,4]{1,0:T(2,128)S(1)} %pad_add_fusion.3.place_ref, bf16[256,512]{1,0:T(8,128)(2,1)S(1)} %get-tuple-element.17.refs_6_.refs_0_, bf16[256,512]{1,0:T(8,128)(2,1)S(1)} %collective-permute-done.3.refs_1_, bf16[256,512]{1,0:T(8,128)(2,1)S(1)} %collective-permute-done.4.refs_2_, ...), custom_call_target="tpu_custom_call" | custom-call | flops 4294967296 | bytes 4194304 | tf_op jit(solution)/shard_map/frame_attention/pallas_call | solution.py:213
  68.1 9.4 %all-to-all-start = ((bf16[128,16,512]{2,1,0:T(8,128)(2,1)}), bf16[128,16,512]{2,1,0:T(8,128)(2,1)S(1)}, u32[]{:S(2)}, u32[]{:S(2)}) async-start(bf16[128,16,512]{2,1,0:T(8,128)(2,1)} %bitcast.19), calls=%async_computation | async-start | bytes 4194304 | tf_op jit(solution)/shard_map/all_to_all | solution.py:333
  77.5 0.1 fusion.1.bias_ref
  77.6 29.5 %all-to-all-done = bf16[128,16,512]{2,1,0:T(8,128)(2,1)S(1)} async-done(((bf16[128,16,512]{2,1,0:T(8,128)(2,1)}), bf16[128,16,512]{2,1,0:T(8,128)(2,1)S(1)}, u32[]{:S(2)}, u32[]{:S(2)}) %all-to-all-start) | async-done | bytes 2097184 | tf_op jit(solution)/shard_map/all_to_all | solution.py:333
  107.1 0.0 copy-start.4
  107.2 1.6 %copy-done.4 = bf16[4,512,512]{2,1,0:T(8,128)(2,1)S(1)} copy-done((bf16[4,512,512]{2,1,0:T(8,128)(2,1)S(1)}, bf16[4,512,512]{2,1,0:T(8,128)(2,1)}, u32[]{:S(2)}) %copy-start.4) | copy-done | bytes 2097176
  108.7 8.6 %time_attention.1 = bf16[256,4,2,512]{3,2,1,0:T(2,128)(2,1)} custom-call(bf16[8,256,512]{2,1,0:T(8,128)(2,1)S(1)} %bitcast.43, f32[256,256]{1,0:T(8,128)S(1)} %fusion.1.bias_ref, bf16[4,512,512]{2,1,0:T(8,128)(2,1)S(1)} %copy-done.4), custom_call_target="tpu_custom_call" | custom-call | flops 5368709120 | bytes 6291456 | tf_op jit(solution)/shard_map/time_attention/pallas_call | solution.py:273
  (13 shorter events, 0.1 us)
Async XLA Ops:
  0.0 9.9 %copy-start = (bf16[16,4,32,512]{3,2,1,0:T(8,128)(2,1)S(1)}, bf16[16,4,32,512]{3,2,1,0:T(8,128)(2,1)}, u32[]{:S(2)}) copy-start(bf16[16,4,32,512]{3,2,1,0:T(8,128)(2,1)} %param.6) | copy-start | bytes 6291460
  0.0 9.1 %copy-start.6 = (s32[256]{0:T(256)S(1)}, s32[256]{0:T(256)}, u32[]{:S(2)}) copy-start(s32[256]{0:T(256)} %param.7) | copy-start | bytes 3076
  2.5 15.1 %collective-permute-start = (bf16[16,32,512]{2,1,0:T(8,128)(2,1)}, bf16[16,32,512]{2,1,0:T(8,128)(2,1)S(1)}, u32[]{:S(2)}, u32[]{:S(2)}) collective-permute-start(bf16[16,32,512]{2,1,0:T(8,128)(2,1)} %get-tuple-element.30), channel_id=1, source_target_pairs={{0,1},{1,2},{2,3},{3,4},{4,5},{5,6},{6,7},{8,9},{9,10},{10,11},{11... | collective-permute-start | bytes 1572872 | tf_op jit(solution)/shard_map/ppermute | solution.py:299
  7.0 10.7 %collective-permute-start.1 = (bf16[16,32,512]{2,1,0:T(8,128)(2,1)}, bf16[16,32,512]{2,1,0:T(8,128)(2,1)S(1)}, u32[]{:S(2)}, u32[]{:S(2)}) collective-permute-start(bf16[16,32,512]{2,1,0:T(8,128)(2,1)} %get-tuple-element.29), channel_id=1, source_target_pairs={{1,0},{2,1},{3,2},{4,3},{5,4},{6,5},{7,6},{9,8},{10,9},{11,10},{12... | collective-permute-start | bytes 1572872 | tf_op jit(solution)/shard_map/ppermute | solution.py:300
  9.9 2.3 %copy-start.1 = (bf16[9,512,512]{2,1,0:T(8,128)(2,1)S(1)}, bf16[9,512,512]{2,1,0:T(8,128)(2,1)}, u32[]{:S(2)}) copy-start(bf16[9,512,512]{2,1,0:T(8,128)(2,1)} %refs_2_.1) | copy-start | bytes 14155780
  12.2 5.5 %copy-start.5 = (bf16[3,512,512]{2,1,0:T(8,128)(2,1)S(1)}, bf16[3,512,512]{2,1,0:T(8,128)(2,1)}, u32[]{:S(2)}) copy-start(bf16[3,512,512]{2,1,0:T(8,128)(2,1)} %refs_3_.1) | copy-start | bytes 4718596
  17.8 14.5 %copy-start.2 = (bf16[9,512,512]{2,1,0:T(8,128)(2,1)S(1)}, bf16[9,512,512]{2,1,0:T(8,128)(2,1)}, u32[]{:S(2)}) copy-start(bf16[9,512,512]{2,1,0:T(8,128)(2,1)} %refs_2_.1) | copy-start | bytes 14155780
  23.9 8.3 %collective-permute-start.2 = (bf16[2,128,512]{2,1,0:T(8,128)(2,1)S(1)}, bf16[2,128,512]{2,1,0:T(8,128)(2,1)S(1)}, u32[]{:S(2)}, u32[]{:S(2)}) collective-permute-start(bf16[2,128,512]{2,1,0:T(8,128)(2,1)S(1)} %get-tuple-element.16), channel_id=1, source_target_pairs={{0,8},{8,16},{16,24},{24,32},{32,40},{40,48},{48,56},{56,64},{64,7... | collective-permute-start | bytes 786440 | tf_op jit(solution)/shard_map/ppermute | solution.py:328
  27.5 19.4 %collective-permute-start.7 = (bf16[256,512]{1,0:T(8,128)(2,1)S(1)}, bf16[256,512]{1,0:T(8,128)(2,1)S(1)}, u32[]{:S(2)}, u32[]{:S(2)}) collective-permute-start(bf16[256,512]{1,0:T(8,128)(2,1)S(1)} %get-tuple-element.22), channel_id=1, source_target_pairs={{0,2},{2,4},{4,6},{6,0},{1,3},{3,5},{5,7},{7,1},{8,10},{10,12},{12... | collective-permute-start | bytes 786440 | tf_op jit(solution)/shard_map/ppermute | solution.py:324
  28.8 18.0 %collective-permute-start.8 = (bf16[256,512]{1,0:T(8,128)(2,1)S(1)}, bf16[256,512]{1,0:T(8,128)(2,1)S(1)}, u32[]{:S(2)}, u32[]{:S(2)}) collective-permute-start(bf16[256,512]{1,0:T(8,128)(2,1)S(1)} %get-tuple-element.23), channel_id=1, source_target_pairs={{0,4},{2,6},{4,0},{6,2},{1,5},{3,7},{5,1},{7,3},{8,12},{10,14},{12... | collective-permute-start | bytes 786440 | tf_op jit(solution)/shard_map/ppermute | solution.py:324
  30.3 12.6 %collective-permute-start.9 = (bf16[256,512]{1,0:T(8,128)(2,1)S(1)}, bf16[256,512]{1,0:T(8,128)(2,1)S(1)}, u32[]{:S(2)}, u32[]{:S(2)}) collective-permute-start(bf16[256,512]{1,0:T(8,128)(2,1)S(1)} %get-tuple-element.24), channel_id=1, source_target_pairs={{0,6},{2,0},{4,2},{6,4},{1,7},{3,1},{5,3},{7,5},{8,14},{10,8},{12,... | collective-permute-start | bytes 786440 | tf_op jit(solution)/shard_map/ppermute | solution.py:324
  37.1 18.1 %copy-start.3 = (bf16[4,512,512]{2,1,0:T(8,128)(2,1)S(1)}, bf16[4,512,512]{2,1,0:T(8,128)(2,1)}, u32[]{:S(2)}) copy-start(bf16[4,512,512]{2,1,0:T(8,128)(2,1)} %refs_5_.3) | copy-start | bytes 6291460
  37.1 16.3 %collective-permute-start.3 = (bf16[256,512]{1,0:T(8,128)(2,1)S(1)}, bf16[256,512]{1,0:T(8,128)(2,1)S(1)}, u32[]{:S(2)}, u32[]{:S(2)}) collective-permute-start(bf16[256,512]{1,0:T(8,128)(2,1)S(1)} %get-tuple-element.18), channel_id=1, source_target_pairs={{0,2},{2,4},{4,6},{6,0},{1,3},{3,5},{5,7},{7,1},{8,10},{10,12},{12... | collective-permute-start | bytes 786440 | tf_op jit(solution)/shard_map/ppermute | solution.py:324
  38.9 14.5 %collective-permute-start.4 = (bf16[256,512]{1,0:T(8,128)(2,1)S(1)}, bf16[256,512]{1,0:T(8,128)(2,1)S(1)}, u32[]{:S(2)}, u32[]{:S(2)}) collective-permute-start(bf16[256,512]{1,0:T(8,128)(2,1)S(1)} %get-tuple-element.19), channel_id=1, source_target_pairs={{0,4},{2,6},{4,0},{6,2},{1,5},{3,7},{5,1},{7,3},{8,12},{10,14},{12... | collective-permute-start | bytes 786440 | tf_op jit(solution)/shard_map/ppermute | solution.py:324
  42.9 10.5 %collective-permute-start.5 = (bf16[256,512]{1,0:T(8,128)(2,1)S(1)}, bf16[256,512]{1,0:T(8,128)(2,1)S(1)}, u32[]{:S(2)}, u32[]{:S(2)}) collective-permute-start(bf16[256,512]{1,0:T(8,128)(2,1)S(1)} %get-tuple-element.20), channel_id=1, source_target_pairs={{0,6},{2,0},{4,2},{6,4},{1,7},{3,1},{5,3},{7,5},{8,14},{10,8},{12,... | collective-permute-start | bytes 786440 | tf_op jit(solution)/shard_map/ppermute | solution.py:324
  46.9 8.3 %collective-permute-start.10 = (bf16[4,128,512]{2,1,0:T(8,128)(2,1)S(1)}, bf16[4,128,512]{2,1,0:T(8,128)(2,1)S(1)}, u32[]{:S(2)}, u32[]{:S(2)}) collective-permute-start(bf16[4,128,512]{2,1,0:T(8,128)(2,1)S(1)} %pad_maximum_fusion.1), channel_id=1, source_target_pairs={{0,1},{1,0},{2,3},{3,2},{4,5},{5,4},{6,7},{7,6},{8,9},{9,8},{10,11... | collective-permute-start | bytes 1572872 | tf_op jit(solution)/shard_map/ppermute | solution.py:297
  53.5 7.5 %collective-permute-start.6 = (bf16[4,128,512]{2,1,0:T(8,128)(2,1)S(1)}, bf16[4,128,512]{2,1,0:T(8,128)(2,1)S(1)}, u32[]{:S(2)}, u32[]{:S(2)}) collective-permute-start(bf16[4,128,512]{2,1,0:T(8,128)(2,1)S(1)} %pad_maximum_fusion), channel_id=1, source_target_pairs={{0,1},{1,0},{2,3},{3,2},{4,5},{5,4},{6,7},{7,6},{8,9},{9,8},{10,11... | collective-permute-start | bytes 1572872 | tf_op jit(solution)/shard_map/ppermute | solution.py:297
  68.1 39.0 %all-to-all-start = ((bf16[128,16,512]{2,1,0:T(8,128)(2,1)}), bf16[128,16,512]{2,1,0:T(8,128)(2,1)S(1)}, u32[]{:S(2)}, u32[]{:S(2)}) async-start(bf16[128,16,512]{2,1,0:T(8,128)(2,1)} %bitcast.19), calls=%async_computation | async-start | bytes 4194304 | tf_op jit(solution)/shard_map/all_to_all | solution.py:333
  107.1 1.6 %copy-start.4 = (bf16[4,512,512]{2,1,0:T(8,128)(2,1)S(1)}, bf16[4,512,512]{2,1,0:T(8,128)(2,1)}, u32[]{:S(2)}) copy-start(bf16[4,512,512]{2,1,0:T(8,128)(2,1)} %w_ref.3) | copy-start | bytes 6291460

commit v4 on v3

--- a/solution.py
+++ b/solution.py
@@ -30,30 +30,39 @@
     return jnp.where(in_row == source_of(out_row), 1.0, 0.0).astype(BF)
 
 
-def space_taps(blocks, rows, lhs_of, w_ref, acc, store):
+def space_taps(blocks, rows, lhs_of, w_of, acc, store):
     c = acc.shape[-1]
     row = lax.broadcasted_iota(jnp.int32, (rows, c), 0) & 31
 
-    def product(block, col):
-        weights = jnp.concatenate([w_ref[3 * a + col] for a in range(3)], axis=0)
+    def product(block, weights):
         return mm(lhs_of(block), weights)
 
     def span(block):
         return slice(block * rows, (block + 1) * rows)
 
+    weights = w_of(0)
     for block in range(blocks):
-        acc[span(block)] = jnp.where(row == 0, 0.0, pltpu.roll(product(block, 0), 1, 0))
+        acc[span(block)] = jnp.where(row == 0, 0.0, pltpu.roll(product(block, weights), 1, 0))
+    weights = w_of(1)
     for block in range(blocks):
-        acc[span(block)] += product(block, 1)
+        acc[span(block)] += product(block, weights)
+    weights = w_of(2)
     for block in range(blocks):
-        v = acc[span(block)] + jnp.where(row == 31, 0.0, pltpu.roll(product(block, 2), rows - 1, 0))
+        v = acc[span(block)] + jnp.where(row == 31, 0.0, pltpu.roll(product(block, weights), rows - 1, 0))
         half = 0.5 * v
         store(block, (half + half * jnp.tanh(half)).astype(BF))
 
 
-def inner_kernel(x_ref, w_ref, out_ref, acc):
+def inner_kernel(x_ref, w_ref, out_ref, acc, w_s, sems):
     frames, tokens, c = out_ref.shape
     per = 8
+    copies = [pltpu.make_async_copy(w_ref.at[:, col], w_s.at[col], sems.at[col]) for col in range(3)]
+    for copy in copies:
+        copy.start()
+
+    def w_of(col):
+        copies[col].wait()
+        return w_s[col].reshape(3 * c, c)
 
     def lhs_of(block):
         f = slice(block * per, (block + 1) * per)
@@ -64,7 +73,7 @@
     def store(block, hidden):
         out_ref[block * per : (block + 1) * per] = hidden.reshape(per, tokens, c)
 
-    space_taps(frames // per, per * tokens, lhs_of, w_ref, acc, store)
+    space_taps(frames // per, per * tokens, lhs_of, w_of, acc, store)
 
 
 def conv_inner(x, w_space):
@@ -74,13 +83,17 @@
     return pl.pallas_call(
         inner_kernel,
         out_shape=jax.ShapeDtypeStruct((frames, tokens - 64, c), BF),
-        in_specs=[vmem] * 2,
+        in_specs=[vmem, pl.BlockSpec(memory_space=pltpu.HBM)],
         out_specs=vmem,
-        scratch_shapes=[pltpu.VMEM((rows, c), F32)],
+        scratch_shapes=[
+            pltpu.VMEM((rows, c), F32),
+            pltpu.VMEM((3, 3, c, c), BF),
+            pltpu.SemaphoreType.DMA((3,)),
+        ],
         compiler_params=pltpu.CompilerParams(vmem_limit_bytes=VMEM_LIMIT),
         cost_estimate=pl.CostEstimate(flops=18 * rows * c * c, bytes_accessed=8 * 2**20, transcendentals=0),
         name="conv_inner",
-    )(x, w_space)
+    )(x, pltpu.with_memory_space_constraint(w_space.reshape(3, 3, c, c), pltpu.HBM))
 
 
 def outer_kernel(late, idx_ref, x_ref, up_ref, dn_ref, inner_ref, *refs):
@@ -112,7 +125,10 @@
         hs[here, 0:32, :] = hidden[0]
         hs[here, 96:128, :] = hidden[1]
 
-    space_taps(1, rows, lhs_of, w_ref, acc, store)
+    def w_of(col):
+        return jnp.concatenate([w_ref[3 * a + col] for a in range(3)], axis=0)
+
+    space_taps(1, rows, lhs_of, w_of, acc, store)
 
     order = one_hot_rows(128, lambda o: ((o >> 1) & 3) * 32 + (o >> 3) * 2 + (o & 1))
     weights = wt_ref[...].reshape(3 * c, c)

time: 118 us -> 118 us (level)
  local copies, waits for them, and re-layouts: 6.78 us -> 4.46 us
  Pallas kernels: 37.8 us -> 39.8 us
    unnamed x14 -> x12, local copies, waits for them, and re-layouts: 3.94 us -> 1.62 us
    pallas_call x1, Pallas kernels: 5.37 us -> 7.29 us  [conv_inner(): pl.pallas_call(inner_kernel, out_shape=jax.ShapeDtypeStruct((frames, toke...]
  transfers between devices with their start and end apart: 12 -> 12, of which waited for: 4 -> 4; matrix products, arithmetic and copies ran while one was open for 1% -> 1% of each run, Pallas kernels for 14% -> 15%
where the time goes in v4:
time: 118 us; the launch traced here: 117 us
  Pallas kernels  39.8 us (34%)
  waiting for transfers between devices  38.1 us (32%)
  starting transfers between devices  34 us (29%)
  local copies, waits for them, and re-layouts  4.46 us (4%)
    all_to_all x1, waiting for transfers between devices, shards(): lax.all_to_all(done.reshape(row_count * tm_count, -1, c), ('y', 'core', '...  29.5 us
    pallas_call x2, Pallas kernels, frame_attention(): pl.pallas_call(functools.partial(frame_kernel, pair), out_shape=jax.Shape...  12.8 us
    ppermute x6, starting transfers between devices, exchanged(): lax.ppermute(blocks[s], 'y', turn(s))  12 us
    pallas_call x2, Pallas kernels, conv_outer(): pl.pallas_call(functools.partial(outer_kernel, late), out_shape=out_shape...  11 us
    all_to_all x1, starting transfers between devices, shards(): lax.all_to_all(done.reshape(row_count * tm_count, -1, c), ('y', 'core', '...  9.41 us
    pallas_call x1, Pallas kernels, time_attention(): pl.pallas_call(time_kernel, out_shape=jax.ShapeDtypeStruct((256, 4, 2, c)...  8.64 us
    ppermute x6, waiting for transfers between devices, exchanged(): lax.ppermute(blocks[s], 'y', turn(s))  8.01 us
    pallas_call x1, Pallas kernels, conv_inner(): pl.pallas_call(inner_kernel, out_shape=jax.ShapeDtypeStruct((frames, toke...  7.29 us
  transfers between devices with their start and end apart: 12, of which 4 were waited for; matrix products, arithmetic and copies ran while one was open for 1% of the time, Pallas kernels for 15%

profile of v4, /device:TPU:1, one launch (start us, length us, event | category | flops | bytes accessed | tf_op | source)
XLA Modules:
  0.0 117.4 jit_solution(15675842649664630351)
XLA Ops:
  0.0 0.0 copy-start
  0.0 0.0 copy-start.5
  0.0 2.5 %slice_bitcast_fusion = (bf16[16,32,512]{2,1,0:T(8,128)(2,1)}, bf16[16,32,512]{2,1,0:T(8,128)(2,1)}) fusion(bf16[16,4,32,512]{3,2,1,0:T(8,128)(2,1)} %param.6), kind=kLoop, calls=%fused_computation.2 | loop fusion | bytes 2097152 | tf_op jit(solution)/shard_map/squeeze | solution.py:316
  2.5 4.6 %collective-permute-start = (bf16[16,32,512]{2,1,0:T(8,128)(2,1)}, bf16[16,32,512]{2,1,0:T(8,128)(2,1)S(1)}, u32[]{:S(2)}, u32[]{:S(2)}) collective-permute-start(bf16[16,32,512]{2,1,0:T(8,128)(2,1)} %get-tuple-element.30), channel_id=1, source_target_pairs={{0,1},{1,2},{2,3},{3,4},{4,5},{5,6},{6,7},{8,9},{9,10},{10,11},{11... | collective-permute-start | bytes 1572872 | tf_op jit(solution)/shard_map/ppermute | solution.py:315
  7.0 1.9 %collective-permute-start.1 = (bf16[16,32,512]{2,1,0:T(8,128)(2,1)}, bf16[16,32,512]{2,1,0:T(8,128)(2,1)S(1)}, u32[]{:S(2)}, u32[]{:S(2)}) collective-permute-start(bf16[16,32,512]{2,1,0:T(8,128)(2,1)} %get-tuple-element.29), channel_id=1, source_target_pairs={{1,0},{2,1},{3,2},{4,3},{5,4},{6,5},{7,6},{9,8},{10,9},{11,10},{12... | collective-permute-start | bytes 1572872 | tf_op jit(solution)/shard_map/ppermute | solution.py:316
  9.0 0.1 add_bitcast_fusion.2
  9.1 0.0 copy-done.5
  9.1 0.1 pad_dynamic-slice_fusion
  9.2 0.1 compare_select_fusion.2
  9.2 0.1 slice_bitcast_fusion.12
  9.3 0.1 slice_bitcast_fusion.13
  9.4 0.1 pad_add_fusion
  9.5 0.1 eq.24
  9.6 0.1 iota_compare_fusion.1
  9.6 0.2 select_reduce_fusion
  9.9 0.0 copy-done
  9.9 0.0 copy-start.1
  9.9 0.0 copy-start.4
  9.9 7.3 %conv_inner.1.inner_ref = bf16[16,64,512]{2,1,0:T(8,128)(2,1)S(1)} custom-call(bf16[16,128,512]{2,1,0:T(8,128)(2,1)S(1)} %bitcast.45, bf16[3,3,512,512]{3,2,1,0:T(8,128)(2,1)} %bitcast.48), custom_call_target="tpu_custom_call" | custom-call | flops 4831838208 | bytes 8388608 | tf_op jit(solution)/shard_map/conv_inner/pallas_call | solution.py:83
  17.2 0.0 collective-permute-done.up_ref
  17.2 0.6 collective-permute-done.1.dn_ref
  17.8 0.0 copy-done.1
  17.8 0.0 copy-done.4
  17.8 6.2 %conv_outer.2 = (bf16[256,512]{1,0:T(8,128)(2,1)S(1)}, bf16[256,512]{1,0:T(8,128)(2,1)S(1)}, bf16[256,512]{1,0:T(8,128)(2,1)S(1)}, bf16[256,512]{1,0:T(8,128)(2,...) custom-call(s32[4,8]{1,0:T(4,128)S(1)} %get-tuple-element.25.idx_ref, ...), custom_call_target="tpu_custom_call" | custom-call | flops 4630511616 | bytes 9437184 | tf_op jit(solution)/shard_map/conv_outer/pallas_call | solution.py:157
  23.9 3.6 %collective-permute-start.2 = (bf16[2,128,512]{2,1,0:T(8,128)(2,1)S(1)}, bf16[2,128,512]{2,1,0:T(8,128)(2,1)S(1)}, u32[]{:S(2)}, u32[]{:S(2)}) collective-permute-start(bf16[2,128,512]{2,1,0:T(8,128)(2,1)S(1)} %get-tuple-element.16), channel_id=1, source_target_pairs={{0,8},{8,16},{16,24},{24,32},{32,40},{40,48},{48,56},{56,64},{64,7... | collective-permute-start | bytes 786440 | tf_op jit(solution)/shard_map/ppermute | solution.py:344
  27.5 1.4 %collective-permute-start.7 = (bf16[256,512]{1,0:T(8,128)(2,1)S(1)}, bf16[256,512]{1,0:T(8,128)(2,1)S(1)}, u32[]{:S(2)}, u32[]{:S(2)}) collective-permute-start(bf16[256,512]{1,0:T(8,128)(2,1)S(1)} %get-tuple-element.22), channel_id=1, source_target_pairs={{0,2},{2,4},{4,6},{6,0},{1,3},{3,5},{5,7},{7,1},{8,10},{10,12},{12... | collective-permute-start | bytes 786440 | tf_op jit(solution)/shard_map/ppermute | solution.py:340
  28.9 1.4 %collective-permute-start.8 = (bf16[256,512]{1,0:T(8,128)(2,1)S(1)}, bf16[256,512]{1,0:T(8,128)(2,1)S(1)}, u32[]{:S(2)}, u32[]{:S(2)}) collective-permute-start(bf16[256,512]{1,0:T(8,128)(2,1)S(1)} %get-tuple-element.23), channel_id=1, source_target_pairs={{0,4},{2,6},{4,0},{6,2},{1,5},{3,7},{5,1},{7,3},{8,12},{10,14},{12... | collective-permute-start | bytes 786440 | tf_op jit(solution)/shard_map/ppermute | solution.py:340
  30.3 2.0 %collective-permute-start.9 = (bf16[256,512]{1,0:T(8,128)(2,1)S(1)}, bf16[256,512]{1,0:T(8,128)(2,1)S(1)}, u32[]{:S(2)}, u32[]{:S(2)}) collective-permute-start(bf16[256,512]{1,0:T(8,128)(2,1)S(1)} %get-tuple-element.24), channel_id=1, source_target_pairs={{0,6},{2,0},{4,2},{6,4},{1,7},{3,1},{5,3},{7,5},{8,14},{10,8},{12,... | collective-permute-start | bytes 786440 | tf_op jit(solution)/shard_map/ppermute | solution.py:340
  32.3 0.0 collective-permute-done.2.refs_1_
  32.3 4.8 %conv_outer.3 = (bf16[256,512]{1,0:T(8,128)(2,1)S(1)}, bf16[256,512]{1,0:T(8,128)(2,1)S(1)}, bf16[256,512]{1,0:T(8,128)(2,1)S(1)}, bf16[256,512]{1,0:T(8,128)(2,1)S(1)}) custom-call(s32[4,8]{1,0:T(4,128)S(1)} %get-tuple-element.26.idx_ref, bf16[16,128,512]{2,1,0:T(8,128)(2,1)S(1)} %bitcast.47, bf16[16,32,512]{2,1,0:T(8,128)(2,1)S(1)} %collective-permute-done.up_ref, ...), custom_call_target="tpu_custom_call" | custom-call | flops 3422552064 | bytes 9437184 | tf_op jit(solution)/shard_map/conv_outer/pallas_call | solution.py:157
  37.1 0.0 copy-start.2
  37.1 2.3 %collective-permute-start.3 = (bf16[256,512]{1,0:T(8,128)(2,1)S(1)}, bf16[256,512]{1,0:T(8,128)(2,1)S(1)}, u32[]{:S(2)}, u32[]{:S(2)}) collective-permute-start(bf16[256,512]{1,0:T(8,128)(2,1)S(1)} %get-tuple-element.18), channel_id=1, source_target_pairs={{0,2},{2,4},{4,6},{6,0},{1,3},{3,5},{5,7},{7,1},{8,10},{10,12},{12... | collective-permute-start | bytes 786440 | tf_op jit(solution)/shard_map/ppermute | solution.py:340
  39.4 1.1 collective-permute-start.4
  40.5 2.0 %collective-permute-done.9.refs_3_ = bf16[256,512]{1,0:T(8,128)(2,1)S(1)} collective-permute-done((bf16[256,512]{1,0:T(8,128)(2,1)S(1)}, bf16[256,512]{1,0:T(8,128)(2,1)S(1)}, u32[]{:S(2)}, u32[]{:S(2)}) %collective-permute-start.9) | collective-permute-done | bytes 262176 | tf_op jit(solution)/shard_map/ppermute | solution.py:340
  42.4 3.9 %collective-permute-start.5 = (bf16[256,512]{1,0:T(8,128)(2,1)S(1)}, bf16[256,512]{1,0:T(8,128)(2,1)S(1)}, u32[]{:S(2)}, u32[]{:S(2)}) collective-permute-start(bf16[256,512]{1,0:T(8,128)(2,1)S(1)} %get-tuple-element.20), channel_id=1, source_target_pairs={{0,6},{2,0},{4,2},{6,4},{1,7},{3,1},{5,3},{7,5},{8,14},{10,8},{12,... | collective-permute-start | bytes 786440 | tf_op jit(solution)/shard_map/ppermute | solution.py:340
  46.4 0.0 collective-permute-done.8.refs_2_
  46.4 0.0 collective-permute-done.7.refs_1_
  46.4 0.1 pad_maximum_fusion.1
  46.5 1.1 collective-permute-start.10
  47.6 6.0 %collective-permute-done.5.refs_3_ = bf16[256,512]{1,0:T(8,128)(2,1)S(1)} collective-permute-done((bf16[256,512]{1,0:T(8,128)(2,1)S(1)}, bf16[256,512]{1,0:T(8,128)(2,1)S(1)}, u32[]{:S(2)}, u32[]{:S(2)}) %collective-permute-start.5) | collective-permute-done | bytes 262176 | tf_op jit(solution)/shard_map/ppermute | solution.py:340
  53.7 0.0 collective-permute-done.4.refs_2_
  53.7 0.0 collective-permute-done.3.refs_1_
  53.7 0.1 pad_maximum_fusion
  53.8 1.4 %collective-permute-start.6 = (bf16[4,128,512]{2,1,0:T(8,128)(2,1)S(1)}, bf16[4,128,512]{2,1,0:T(8,128)(2,1)S(1)}, u32[]{:S(2)}, u32[]{:S(2)}) collective-permute-start(bf16[4,128,512]{2,1,0:T(8,128)(2,1)S(1)} %pad_maximum_fusion), channel_id=1, source_target_pairs={{0,1},{1,0},{2,3},{3,2},{4,5},{5,4},{6,7},{7,6},{8,9},{9,8},{10,11... | collective-permute-start | bytes 1572872 | tf_op jit(solution)/shard_map/ppermute | solution.py:313
  55.2 0.0 collective-permute-done.10.refs_4_
  55.2 0.0 copy-done.2
  55.2 5.8 %frame_attention.2.refs_6_ = bf16[8,128,512]{2,1,0:T(8,128)(2,1)S(1)} custom-call(s32[2,4]{1,0:T(2,128)S(1)} %pad_add_fusion.3.place_ref, bf16[256,512]{1,0:T(8,128)(2,1)S(1)} %get-tuple-element.21.refs_0_, bf16[256,512]{1,0:T(8,128)(2,1)S(1)} %collective-permute-done.7.refs_1_, bf16[256,512]{1,0:T(8,128)(2,1)S(1)} %collective-permute-done.8.refs_2_, ...), custom_call_target="tpu_custom_call" | custom-call | flops 4294967296 | bytes 4194304 | tf_op jit(solution)/shard_map/frame_attention/pallas_call | solution.py:229
  61.0 0.0 collective-permute-done.6.refs_4_
  61.0 7.1 %frame_attention.3 = bf16[8,256,512]{2,1,0:T(8,128)(2,1)} custom-call(s32[2,4]{1,0:T(2,128)S(1)} %pad_add_fusion.3.place_ref, bf16[256,512]{1,0:T(8,128)(2,1)S(1)} %get-tuple-element.17.refs_6_.refs_0_, bf16[256,512]{1,0:T(8,128)(2,1)S(1)} %collective-permute-done.3.refs_1_, bf16[256,512]{1,0:T(8,128)(2,1)S(1)} %collective-permute-done.4.refs_2_, ...), custom_call_target="tpu_custom_call" | custom-call | flops 4294967296 | bytes 4194304 | tf_op jit(solution)/shard_map/frame_attention/pallas_call | solution.py:229
  68.1 9.4 %all-to-all-start = ((bf16[128,16,512]{2,1,0:T(8,128)(2,1)}), bf16[128,16,512]{2,1,0:T(8,128)(2,1)S(1)}, u32[]{:S(2)}, u32[]{:S(2)}) async-start(bf16[128,16,512]{2,1,0:T(8,128)(2,1)} %bitcast.20), calls=%async_computation | async-start | bytes 4194304 | tf_op jit(solution)/shard_map/all_to_all | solution.py:349
  77.5 0.1 fusion.1.bias_ref
  77.6 29.5 %all-to-all-done = bf16[128,16,512]{2,1,0:T(8,128)(2,1)S(1)} async-done(((bf16[128,16,512]{2,1,0:T(8,128)(2,1)}), bf16[128,16,512]{2,1,0:T(8,128)(2,1)S(1)}, u32[]{:S(2)}, u32[]{:S(2)}) %all-to-all-start) | async-done | bytes 2097184 | tf_op jit(solution)/shard_map/all_to_all | solution.py:349
  107.2 0.0 copy-start.3
  107.2 1.6 %copy-done.3 = bf16[4,512,512]{2,1,0:T(8,128)(2,1)S(1)} copy-done((bf16[4,512,512]{2,1,0:T(8,128)(2,1)S(1)}, bf16[4,512,512]{2,1,0:T(8,128)(2,1)}, u32[]{:S(2)}) %copy-start.3) | copy-done | bytes 2097176
  108.8 8.6 %time_attention.1 = bf16[256,4,2,512]{3,2,1,0:T(2,128)(2,1)} custom-call(bf16[8,256,512]{2,1,0:T(8,128)(2,1)S(1)} %bitcast.44, f32[256,256]{1,0:T(8,128)S(1)} %fusion.1.bias_ref, bf16[4,512,512]{2,1,0:T(8,128)(2,1)S(1)} %copy-done.3), custom_call_target="tpu_custom_call" | custom-call | flops 5368709120 | bytes 6291456 | tf_op jit(solution)/shard_map/time_attention/pallas_call | solution.py:289
  (13 shorter events, 0.1 us)
Async XLA Ops:
  0.0 9.9 %copy-start = (bf16[16,4,32,512]{3,2,1,0:T(8,128)(2,1)S(1)}, bf16[16,4,32,512]{3,2,1,0:T(8,128)(2,1)}, u32[]{:S(2)}) copy-start(bf16[16,4,32,512]{3,2,1,0:T(8,128)(2,1)} %param.6) | copy-start | bytes 6291460
  0.0 9.1 %copy-start.5 = (s32[256]{0:T(256)S(1)}, s32[256]{0:T(256)}, u32[]{:S(2)}) copy-start(s32[256]{0:T(256)} %param.7) | copy-start | bytes 3076
  2.5 14.7 %collective-permute-start = (bf16[16,32,512]{2,1,0:T(8,128)(2,1)}, bf16[16,32,512]{2,1,0:T(8,128)(2,1)S(1)}, u32[]{:S(2)}, u32[]{:S(2)}) collective-permute-start(bf16[16,32,512]{2,1,0:T(8,128)(2,1)} %get-tuple-element.30), channel_id=1, source_target_pairs={{0,1},{1,2},{2,3},{3,4},{4,5},{5,6},{6,7},{8,9},{9,10},{10,11},{11... | collective-permute-start | bytes 1572872 | tf_op jit(solution)/shard_map/ppermute | solution.py:315
  7.0 10.7 %collective-permute-start.1 = (bf16[16,32,512]{2,1,0:T(8,128)(2,1)}, bf16[16,32,512]{2,1,0:T(8,128)(2,1)S(1)}, u32[]{:S(2)}, u32[]{:S(2)}) collective-permute-start(bf16[16,32,512]{2,1,0:T(8,128)(2,1)} %get-tuple-element.29), channel_id=1, source_target_pairs={{1,0},{2,1},{3,2},{4,3},{5,4},{6,5},{7,6},{9,8},{10,9},{11,10},{12... | collective-permute-start | bytes 1572872 | tf_op jit(solution)/shard_map/ppermute | solution.py:316
  9.9 7.9 %copy-start.1 = (bf16[9,512,512]{2,1,0:T(8,128)(2,1)S(1)}, bf16[9,512,512]{2,1,0:T(8,128)(2,1)}, u32[]{:S(2)}) copy-start(bf16[9,512,512]{2,1,0:T(8,128)(2,1)} %refs_2_.1) | copy-start | bytes 14155780
  9.9 7.9 %copy-start.4 = (bf16[3,512,512]{2,1,0:T(8,128)(2,1)S(1)}, bf16[3,512,512]{2,1,0:T(8,128)(2,1)}, u32[]{:S(2)}) copy-start(bf16[3,512,512]{2,1,0:T(8,128)(2,1)} %refs_3_.1) | copy-start | bytes 4718596
  23.9 8.3 %collective-permute-start.2 = (bf16[2,128,512]{2,1,0:T(8,128)(2,1)S(1)}, bf16[2,128,512]{2,1,0:T(8,128)(2,1)S(1)}, u32[]{:S(2)}, u32[]{:S(2)}) collective-permute-start(bf16[2,128,512]{2,1,0:T(8,128)(2,1)S(1)} %get-tuple-element.16), channel_id=1, source_target_pairs={{0,8},{8,16},{16,24},{24,32},{32,40},{40,48},{48,56},{56,64},{64,7... | collective-permute-start | bytes 786440 | tf_op jit(solution)/shard_map/ppermute | solution.py:344
  27.5 18.9 %collective-permute-start.7 = (bf16[256,512]{1,0:T(8,128)(2,1)S(1)}, bf16[256,512]{1,0:T(8,128)(2,1)S(1)}, u32[]{:S(2)}, u32[]{:S(2)}) collective-permute-start(bf16[256,512]{1,0:T(8,128)(2,1)S(1)} %get-tuple-element.22), channel_id=1, source_target_pairs={{0,2},{2,4},{4,6},{6,0},{1,3},{3,5},{5,7},{7,1},{8,10},{10,12},{12... | collective-permute-start | bytes 786440 | tf_op jit(solution)/shard_map/ppermute | solution.py:340
  28.9 17.5 %collective-permute-start.8 = (bf16[256,512]{1,0:T(8,128)(2,1)S(1)}, bf16[256,512]{1,0:T(8,128)(2,1)S(1)}, u32[]{:S(2)}, u32[]{:S(2)}) collective-permute-start(bf16[256,512]{1,0:T(8,128)(2,1)S(1)} %get-tuple-element.23), channel_id=1, source_target_pairs={{0,4},{2,6},{4,0},{6,2},{1,5},{3,7},{5,1},{7,3},{8,12},{10,14},{12... | collective-permute-start | bytes 786440 | tf_op jit(solution)/shard_map/ppermute | solution.py:340
  30.3 12.2 %collective-permute-start.9 = (bf16[256,512]{1,0:T(8,128)(2,1)S(1)}, bf16[256,512]{1,0:T(8,128)(2,1)S(1)}, u32[]{:S(2)}, u32[]{:S(2)}) collective-permute-start(bf16[256,512]{1,0:T(8,128)(2,1)S(1)} %get-tuple-element.24), channel_id=1, source_target_pairs={{0,6},{2,0},{4,2},{6,4},{1,7},{3,1},{5,3},{7,5},{8,14},{10,8},{12,... | collective-permute-start | bytes 786440 | tf_op jit(solution)/shard_map/ppermute | solution.py:340
  37.1 18.1 %copy-start.2 = (bf16[4,512,512]{2,1,0:T(8,128)(2,1)S(1)}, bf16[4,512,512]{2,1,0:T(8,128)(2,1)}, u32[]{:S(2)}) copy-start(bf16[4,512,512]{2,1,0:T(8,128)(2,1)} %refs_5_.3) | copy-start | bytes 6291460
  37.1 16.6 %collective-permute-start.3 = (bf16[256,512]{1,0:T(8,128)(2,1)S(1)}, bf16[256,512]{1,0:T(8,128)(2,1)S(1)}, u32[]{:S(2)}, u32[]{:S(2)}) collective-permute-start(bf16[256,512]{1,0:T(8,128)(2,1)S(1)} %get-tuple-element.18), channel_id=1, source_target_pairs={{0,2},{2,4},{4,6},{6,0},{1,3},{3,5},{5,7},{7,1},{8,10},{10,12},{12... | collective-permute-start | bytes 786440 | tf_op jit(solution)/shard_map/ppermute | solution.py:340
  39.4 14.3 %collective-permute-start.4 = (bf16[256,512]{1,0:T(8,128)(2,1)S(1)}, bf16[256,512]{1,0:T(8,128)(2,1)S(1)}, u32[]{:S(2)}, u32[]{:S(2)}) collective-permute-start(bf16[256,512]{1,0:T(8,128)(2,1)S(1)} %get-tuple-element.19), channel_id=1, source_target_pairs={{0,4},{2,6},{4,0},{6,2},{1,5},{3,7},{5,1},{7,3},{8,12},{10,14},{12... | collective-permute-start | bytes 786440 | tf_op jit(solution)/shard_map/ppermute | solution.py:340
  42.4 11.2 %collective-permute-start.5 = (bf16[256,512]{1,0:T(8,128)(2,1)S(1)}, bf16[256,512]{1,0:T(8,128)(2,1)S(1)}, u32[]{:S(2)}, u32[]{:S(2)}) collective-permute-start(bf16[256,512]{1,0:T(8,128)(2,1)S(1)} %get-tuple-element.20), channel_id=1, source_target_pairs={{0,6},{2,0},{4,2},{6,4},{1,7},{3,1},{5,3},{7,5},{8,14},{10,8},{12,... | collective-permute-start | bytes 786440 | tf_op jit(solution)/shard_map/ppermute | solution.py:340
  46.5 8.7 %collective-permute-start.10 = (bf16[4,128,512]{2,1,0:T(8,128)(2,1)S(1)}, bf16[4,128,512]{2,1,0:T(8,128)(2,1)S(1)}, u32[]{:S(2)}, u32[]{:S(2)}) collective-permute-start(bf16[4,128,512]{2,1,0:T(8,128)(2,1)S(1)} %pad_maximum_fusion.1), channel_id=1, source_target_pairs={{0,1},{1,0},{2,3},{3,2},{4,5},{5,4},{6,7},{7,6},{8,9},{9,8},{10,11... | collective-permute-start | bytes 1572872 | tf_op jit(solution)/shard_map/ppermute | solution.py:313
  53.8 7.2 %collective-permute-start.6 = (bf16[4,128,512]{2,1,0:T(8,128)(2,1)S(1)}, bf16[4,128,512]{2,1,0:T(8,128)(2,1)S(1)}, u32[]{:S(2)}, u32[]{:S(2)}) collective-permute-start(bf16[4,128,512]{2,1,0:T(8,128)(2,1)S(1)} %pad_maximum_fusion), channel_id=1, source_target_pairs={{0,1},{1,0},{2,3},{3,2},{4,5},{5,4},{6,7},{7,6},{8,9},{9,8},{10,11... | collective-permute-start | bytes 1572872 | tf_op jit(solution)/shard_map/ppermute | solution.py:313
  68.1 39.1 %all-to-all-start = ((bf16[128,16,512]{2,1,0:T(8,128)(2,1)}), bf16[128,16,512]{2,1,0:T(8,128)(2,1)S(1)}, u32[]{:S(2)}, u32[]{:S(2)}) async-start(bf16[128,16,512]{2,1,0:T(8,128)(2,1)} %bitcast.20), calls=%async_computation | async-start | bytes 4194304 | tf_op jit(solution)/shard_map/all_to_all | solution.py:349
  107.2 1.6 %copy-start.3 = (bf16[4,512,512]{2,1,0:T(8,128)(2,1)S(1)}, bf16[4,512,512]{2,1,0:T(8,128)(2,1)}, u32[]{:S(2)}) copy-start(bf16[4,512,512]{2,1,0:T(8,128)(2,1)} %w_ref.1) | copy-start | bytes 6291460
